TPU v7x, 32 devices: a whole 2x2x4 slice. The times are simulated.
32 devices in a mesh: row: 4 (over y, core), col: 8 (over z, x).
Axes of the slice: x: 2, y: 2, z: 4, core: 2. Of those that a mesh axis runs over, the one named last changes fastest.
Arguments:
- object_field: float32 [2, 512, 1024], P(None, 'row', 'col'), may hold values from -4 to 4
- probe_modes: float32 [8, 2, 128, 128], replicated, may hold values from -1.5 to 1.5
- coefficients: float32 [4, 8, 32, 8], P('row', 'col'), may hold values from -4 to 4
- offsets: int32 [4, 8, 32, 2], P('row', 'col'), may hold values from 0 to 128
- counts: int32 [4, 8], P('row', 'col'), may hold values from 16 to 32
- measured: int32 [4, 8, 32, 128, 128], P('row', 'col'), may hold values from 0 to 4095
Outputs:
- object_out: float32 [2, 512, 1024], P(None, 'row', 'col')
- modes_out: float32 [8, 2, 128, 128], replicated
- coefficients_out: float32 [4, 8, 32, 8], P('row', 'col')
All inputs are finite; a program needn't handle non-finite values.
Results may differ from a plain program's by a relative error of at most 0.0003.
Values sent between devices are 32-bit elements; how exact they have to be, the bound alone decides.
A program may use at most 128 MiB of HBM per device.

v0:
```python
import math

import jax
import jax.numpy as jnp
from jax import lax
from jax.sharding import PartitionSpec as P

PS = 128
MODES = 8
TILE = 128
PMAX = 32
BLK = 16
ITERS = 2


amp_floor = 0.5
count_scale = 0.03125
highest = lax.Precision.HIGHEST


def extended_2(block, sides, width):
    for axis, dim in sides:
        count = lax.axis_size(axis)
        forward = [(i, i + 1) for i in range(count - 1)]
        backward = [(target, source) for source, target in forward]
        low = lax.ppermute(
            lax.slice_in_dim(block, block.shape[dim] - width, None, axis=dim), axis, forward
        )
        high = lax.ppermute(lax.slice_in_dim(block, 0, width, axis=dim), axis, backward)
        block = jnp.concatenate([low, block, high], axis=dim)
    return block


def dft_tables(length):
    ramp_values = lax.iota(jnp.int32, length)
    phase_index = ramp_values[:, None] * ramp_values[None, :] % length
    angles = phase_index.astype(jnp.float32) * (2.0 * math.pi / length)
    factor = 1.0 / math.sqrt(length)
    return (jnp.cos(angles) * factor, -jnp.sin(angles) * factor)


def left_apply(cos_part, sin_part, real_part, imag_part):
    result_real = jnp.einsum("ab,nbc->nac", cos_part, real_part, precision=highest) - jnp.einsum(
        "ab,nbc->nac", sin_part, imag_part, precision=highest
    )
    result_imag = jnp.einsum("ab,nbc->nac", cos_part, imag_part, precision=highest) + jnp.einsum(
        "ab,nbc->nac", sin_part, real_part, precision=highest
    )
    return (result_real, result_imag)


def right_apply(cos_part, sin_part, real_part, imag_part):
    result_real = jnp.einsum("nab,bc->nac", real_part, cos_part, precision=highest) - jnp.einsum(
        "nab,bc->nac", imag_part, sin_part, precision=highest
    )
    result_imag = jnp.einsum("nab,bc->nac", real_part, sin_part, precision=highest) + jnp.einsum(
        "nab,bc->nac", imag_part, cos_part, precision=highest
    )
    return (result_real, result_imag)


def transform(cos_part, sin_part, real_part, imag_part):
    left_real, left_imag = left_apply(cos_part, sin_part, real_part, imag_part)
    return right_apply(cos_part, sin_part, left_real, left_imag)


def position_terms(patches, coef_rows, in_use, photons, probe_modes, cos_part, sin_part):
    obj_real = patches[:, 0]
    obj_imag = patches[:, 1]
    probes = jnp.einsum("pk,kcxy->pcxy", coef_rows, probe_modes, precision=highest)
    prb_real = probes[:, 0]
    prb_imag = probes[:, 1]
    psi_real = prb_real * obj_real - prb_imag * obj_imag
    psi_imag = prb_real * obj_imag + prb_imag * obj_real
    far_real, far_imag = transform(cos_part, sin_part, psi_real, psi_imag)
    amplitude = jnp.sqrt(far_real * far_real + far_imag * far_imag)
    target = jnp.sqrt(photons.astype(jnp.float32)) * count_scale
    scaling = target / jnp.maximum(amplitude, amp_floor)
    back_real, back_imag = transform(cos_part, -sin_part, far_real * scaling, far_imag * scaling)
    gate_grid = in_use[:, None, None]
    diff_real = (back_real - psi_real) * gate_grid
    diff_imag = (back_imag - psi_imag) * gate_grid
    grad_real = prb_real * diff_real + prb_imag * diff_imag
    grad_imag = prb_real * diff_imag - prb_imag * diff_real
    weight_grid = (prb_real * prb_real + prb_imag * prb_imag) * gate_grid
    cross_real = obj_real * diff_real + obj_imag * diff_imag
    cross_imag = obj_real * diff_imag - obj_imag * diff_real
    obj_power = (obj_real * obj_real + obj_imag * obj_imag) * gate_grid
    used_coef = coef_rows * in_use[:, None]
    moment_real = jnp.einsum("pk,pxy->kxy", used_coef, cross_real, precision=highest)
    moment_imag = jnp.einsum("pk,pxy->kxy", used_coef, cross_imag, precision=highest)
    moment_power = jnp.einsum("pk,pxy->kxy", used_coef * coef_rows, obj_power, precision=highest)
    mode_real = probe_modes[:, 0]
    mode_imag = probe_modes[:, 1]
    numerator = jnp.einsum("pxy,kxy->pk", cross_real, mode_real, precision=highest) + jnp.einsum(
        "pxy,kxy->pk", cross_imag, mode_imag, precision=highest
    )
    denominator = jnp.einsum(
        "pxy,kxy->pk", obj_power, mode_real * mode_real + mode_imag * mode_imag, precision=highest
    )
    coef_new = coef_rows + numerator / (denominator + 1.0)
    pieces = jnp.stack([grad_real, grad_imag, weight_grid], axis=1)
    return (pieces, (moment_real, moment_imag, moment_power), coef_new)


def fold_edges(padded, margin):
    tile_width = padded.shape[1] - 4 * margin
    lower_edge = 2 * margin
    upper_edge = tile_width + 2 * margin
    outer_edge = tile_width + 3 * margin
    inner_end = tile_width - margin
    interior = padded[:, lower_edge:upper_edge, lower_edge:upper_edge]
    interior = interior.at[:, :margin, :].add(padded[:, :margin, lower_edge:upper_edge])
    interior = interior.at[:, inner_end:, :].add(padded[:, outer_edge:, lower_edge:upper_edge])
    interior = interior.at[:, :, :margin].add(padded[:, lower_edge:upper_edge, :margin])
    interior = interior.at[:, :, inner_end:].add(padded[:, lower_edge:upper_edge, outer_edge:])
    interior = interior.at[:, :margin, :margin].add(padded[:, :margin, :margin])
    interior = interior.at[:, :margin, inner_end:].add(padded[:, :margin, outer_edge:])
    interior = interior.at[:, inner_end:, :margin].add(padded[:, outer_edge:, :margin])
    interior = interior.at[:, inner_end:, inner_end:].add(padded[:, outer_edge:, outer_edge:])
    return interior


def selectors(start_index, width, extent):
    pixel_ramp = lax.iota(jnp.int32, width)
    grid_ramp = lax.iota(jnp.int32, extent)
    wanted = start_index[:, None, None] + pixel_ramp[None, :, None]
    return (wanted == grid_ramp[None, None, :]).astype(jnp.float32)


def shards(object_field, probe_modes, coefficients, offsets, counts, measured):
    margin = PS // 2
    extent = TILE + PS
    cos_part, sin_part = dft_tables(PS)
    coef_now = coefficients[0, 0]
    anchor_all = offsets[0, 0]
    count_here = counts[0, 0]
    photon_all = measured[0, 0]
    for iteration in range(ITERS):
        extended = extended_2(object_field, (("row", 1), ("col", 2)), margin)
        modes_now = probe_modes
        coef_start = coef_now

        def run_block(number, running):
            accumulated, moment_real, moment_imag, moment_power, coef_next = running
            first_slot = number * BLK
            anchors = lax.dynamic_slice_in_dim(anchor_all, first_slot, BLK, 0)
            coef_rows = lax.dynamic_slice_in_dim(coef_start, first_slot, BLK, 0)
            photons = lax.dynamic_slice_in_dim(photon_all, first_slot, BLK, 0)
            in_use = (first_slot + lax.iota(jnp.int32, BLK) < count_here).astype(jnp.float32)
            row_select = selectors(anchors[:, 0], PS, extent)
            col_select = selectors(anchors[:, 1], PS, extent)
            row_cut = jnp.einsum("spe,cef->scpf", row_select, extended, precision=highest)
            patches = jnp.einsum("scpf,sqf->scpq", row_cut, col_select, precision=highest)
            pieces, moments, coef_new = position_terms(
                patches, coef_rows, in_use, photons, modes_now, cos_part, sin_part
            )
            placed_cols = jnp.einsum("scpq,sqf->scpf", pieces, col_select, precision=highest)
            accumulated = accumulated + jnp.einsum(
                "spe,scpf->cef", row_select, placed_cols, precision=highest
            )
            coef_next = lax.dynamic_update_slice_in_dim(coef_next, coef_new, first_slot, 0)
            return (
                accumulated,
                moment_real + moments[0],
                moment_imag + moments[1],
                moment_power + moments[2],
                coef_next,
            )

        empty_moment = jnp.zeros((MODES, PS, PS), jnp.float32)
        start_state = (
            jnp.zeros((3, extent, extent), jnp.float32),
            empty_moment,
            empty_moment,
            empty_moment,
            coef_start,
        )
        final_state = lax.fori_loop(0, PMAX // BLK, run_block, start_state)
        accumulated, moment_real, moment_imag, moment_power, coef_now = final_state
        padded = extended_2(accumulated, (("row", 1), ("col", 2)), margin)
        interior = fold_edges(padded, margin)
        object_field = object_field + interior[0:2] / (interior[2:3] + 1.0)
        totals = lax.psum((moment_real, moment_imag, moment_power), ("row", "col"))
        probe_modes = modes_now + jnp.stack([totals[0], totals[1]], axis=1) / (
            totals[2][:, None] + 1.0
        )
    return (object_field, probe_modes, coef_now[None, None])


def solution(mesh):
    placed = (
        P(None, "row", "col"),
        P(),
        P("row", "col", None, None),
        P("row", "col", None, None),
        P("row", "col"),
        P("row", "col", None, None, None),
    )
    return jax.shard_map(
        shards,
        mesh=mesh,
        in_specs=placed,
        out_specs=(P(None, "row", "col"), P(), P("row", "col", None, None)),
        check_vma=False,
    )
```

profile of v0, /device:TPU:5, one launch (start us, length us, event | category | flops | bytes accessed | tf_op | source)
XLA Modules:
  0.0 663.6 jit_solution(15614911350362407269)
XLA Ops:
  14.2 3.1 collective-permute-start.2
  20.8 3.6 collective-permute-done.3
  24.7 162.3 %while.66 = (s32[]{:T(128)}, f32[3,256,256]{1,2,0:T(8,128)}, f32[8,128,128]{2,0,1:T(8,128)}, f32[8,128,128]{2,0,1:T(8,128)}, f32[8,128,128]{2,0,1:T(8,128)}, /*i...) while((s32[]{:T(128)}, f32[3,256,256]{1,2,0:T(8,128)}, ...), condition=%wide.region_1.2_spmd.clone.clone, body=%wide.region_0.1_spmd.clone.clone.sunk | while | flops 18745724928 | bytes 206108528 | solution.py:179
  36.1 2.8 convolution_add_fusion.22
  57.3 2.9 fusion.683
  62.2 3.0 fusion.685
  67.8 3.1 fusion.687
  70.9 2.9 fusion.688
  82.2 2.8 fusion.691
  93.6 3.7 fusion.692
  97.3 3.6 fusion.693
  113.4 3.8 convolution_add_fusion.22
  140.3 3.0 fusion.685
  145.9 3.1 fusion.687
  149.1 2.9 fusion.688
  153.7 3.0 fusion.690
  160.6 2.8 fusion.691
  173.0 3.7 fusion.692
  176.8 3.6 fusion.693
  189.5 6.9 %collective-permute-start.5 = (f32[3,64,256]{1,2,0:T(8,128)S(1)}, f32[3,64,256]{1,2,0:T(8,128)S(1)}, u32[]{:S(2)}, u32[]{:S(2)}) collective-permute-start(f32[3,64,256]{1,2,0:T(8,128)S(1)} %get-tuple-element.1300), channel_id=1, source_target_pairs={{8,0},{16,8},{24,16},{9,1},{17,9},{25,17},{10,2},{18,10},{26,18},{... | collective-permute-start | bytes 589832 | tf_op jit(solution)/shard_map/ppermute | solution.py:29
  202.9 4.6 collective-permute-start.6
  209.3 10.3 %collective-permute-done.6 = f32[3,384,64]{1,2,0:T(8,128)S(1)} collective-permute-done((f32[3,384,64]{1,2,0:T(8,128)S(1)}, f32[3,384,64]{1,2,0:T(8,128)S(1)}, u32[]{:S(2)}, u32[]{:S(2)}) %collective-permute-start.6) | collective-permute-done | bytes 294944 | tf_op jit(solution)/shard_map/ppermute | solution.py:26
  230.2 5.6 collective-permute-start.9
  237.0 4.1 collective-permute-start.10
  243.0 5.4 collective-permute-done.11
  248.8 94.2 %all-reduce.7.cloned.1.call-done = (f32[8,1,128,128]{3,2,1,0:T(8,128)}, f32[8,1,128,128]{3,2,1,0:T(8,128)}, f32[8,128,128]{2,0,1:T(8,128)}) async-done(((f32[8,1,128,128]{3,2,1,0:T(8,128)}, f32[8,1,128,128]{3,2,1,0:T(8,128)}, f32[8,128,128]{2,0,1:T(8,128)}), (f32[8,1,128,128]{3,2,1,0:T(8,128)}, f32[8,1,128,128]{3,2,1,0:T(8,128)}, f32[8,128,128]{2,0,1:T(8,128)})) %all-reduce.7.cloned.1.call-update) | async-done | bytes 1572880 | tf_op jit(solution)/shard_map/psum | solution.py:184
  346.8 161.4 %while.67 = (s32[]{:T(128)}, f32[3,256,256]{1,2,0:T(8,128)}, f32[8,128,128]{2,0,1:T(8,128)}, f32[8,128,128]{2,0,1:T(8,128)}, f32[8,128,128]{2,0,1:T(8,128)}, /*i...) while((s32[]{:T(128)}, f32[3,256,256]{1,2,0:T(8,128)}, ...), condition=%wide.region_7.8_spmd.clone.clone, body=%wide.region_6.7_spmd.clone.clone.sunk | while | flops 18745724928 | bytes 206108528 | solution.py:179
  358.2 2.8 convolution_add_fusion.25
  379.5 2.9 fusion.758
  384.3 2.9 fusion.760
  389.9 3.1 fusion.762
  393.1 3.0 fusion.763
  404.4 2.8 fusion.766
  415.8 3.7 fusion.767
  419.6 3.6 fusion.768
  435.6 3.8 convolution_add_fusion.25
  462.6 2.9 fusion.760
  468.2 3.1 fusion.762
  471.3 3.0 fusion.763
  476.0 3.0 fusion.765
  482.9 2.9 fusion.766
  495.3 3.7 fusion.767
  499.1 3.6 fusion.768
  509.6 3.7 collective-permute-start.13
  521.1 4.7 collective-permute-start.14
  527.6 11.7 %collective-permute-done.14 = f32[3,384,64]{1,2,0:T(8,128)} collective-permute-done((f32[3,384,64]{1,2,0:T(8,128)}, f32[3,384,64]{1,2,0:T(8,128)}, u32[]{:S(2)}, u32[]{:S(2)}) %collective-permute-start.14) | collective-permute-done | bytes 294944 | tf_op jit(solution)/shard_map/ppermute | solution.py:26
  543.0 2.9 add_select_fusion.2
  554.4 98.3 %all-reduce.5.cloned.1.call-done = (f32[8,1,128,128]{3,2,1,0:T(8,128)}, f32[8,1,128,128]{3,2,1,0:T(8,128)}, f32[8,128,128]{2,0,1:T(8,128)}) async-done(((f32[8,1,128,128]{3,2,1,0:T(8,128)}, f32[8,1,128,128]{3,2,1,0:T(8,128)}, f32[8,128,128]{2,0,1:T(8,128)}), (f32[8,1,128,128]{3,2,1,0:T(8,128)}, f32[8,1,128,128]{3,2,1,0:T(8,128)}, f32[8,128,128]{2,0,1:T(8,128)})) %all-reduce.5.cloned.1.call-update) | async-done | bytes 1572880 | tf_op jit(solution)/shard_map/psum | solution.py:184
  (416 shorter events, 274.0 us)
Async XLA Ops:
  7.2 12.9 %copy-start.52 = (s32[3]{0:T(128)S(1)}, s32[3]{0:T(128)}, u32[]{:S(2)}) copy-start(s32[3]{0:T(128)} %constant.531.clone.1) | copy-start | bytes 40
  7.2 6.8 %copy-start.48 = (f32[2,128,128]{2,1,0:T(8,128)S(1)}, f32[2,128,128]{2,1,0:T(8,128)}, u32[]{:S(2)}) copy-start(f32[2,128,128]{2,1,0:T(8,128)} %param.42) | copy-start | bytes 393220
  7.2 12.8 %copy-start.45 = (f32[1,1,32,8]{2,3,1,0:T(8,128)S(1)}, f32[1,1,32,8]{2,3,1,0:T(8,128)}, u32[]{:S(2)}) copy-start(f32[1,1,32,8]{2,3,1,0:T(8,128)} %param.44) | copy-start | bytes 3076
  7.2 335.8 %all-reduce.7.cloned.1.call-start = ((), (), s32[]{:S(2)}) async-start(), calls=%async_computation.1 | async-start | bytes 3145728 | tf_op jit(solution)/shard_map/psum | solution.py:184
  8.1 5.9 collective-permute-start.1
  10.7 14.0 %copy-start.50 = (s32[1,1,32,2]{2,3,1,0:T(2,128)S(1)}, s32[1,1,32,2]{2,3,1,0:T(2,128)}, u32[]{:S(2)}) copy-start(s32[1,1,32,2]{2,3,1,0:T(2,128)} %param.45) | copy-start | bytes 772
  10.7 3.2 collective-permute-start
  14.2 6.6 %collective-permute-start.2 = (f32[2,256,64]{2,1,0:T(8,128)S(1)}, f32[2,256,64]{2,1,0:T(8,128)S(1)}, u32[]{:S(2)}, u32[]{:S(2)}) collective-permute-start(f32[2,256,64]{2,1,0:T(8,128)S(1)} %get-tuple-element.1304), channel_id=1, source_target_pairs={{0,1},{1,2},{2,3},{3,4},{4,5},{5,6},{6,7},{8,9},{9,10},{10,11},{11... | collective-permute-start | bytes 393224 | tf_op jit(solution)/shard_map/ppermute | solution.py:26
  17.3 7.1 %collective-permute-start.3 = (f32[2,256,64]{2,1,0:T(8,128)S(1)}, f32[2,256,64]{2,1,0:T(8,128)S(1)}, u32[]{:S(2)}, u32[]{:S(2)}) collective-permute-start(f32[2,256,64]{2,1,0:T(8,128)S(1)} %get-tuple-element.1305), channel_id=1, source_target_pairs={{1,0},{2,1},{3,2},{4,3},{5,4},{6,5},{7,6},{9,8},{10,9},{11,10},{12... | collective-permute-start | bytes 393224 | tf_op jit(solution)/shard_map/ppermute | solution.py:29
  24.9 8.5 %copy-start.30 = (f32[8,1,128,128]{3,0,2,1:T(8,128)}, f32[8,1,128,128]{3,0,2,1:T(8,128)S(1)}, u32[]{:S(2)}) copy-start(f32[8,1,128,128]{3,0,2,1:T(8,128)S(1)} %get-tuple-element.1574) | copy-start | bytes 1572868 | tf_op jit(solution)/shard_map/while
  27.7 11.1 %copy-start = (f32[16,2,128,128]{3,0,2,1:T(8,128)}, f32[16,2,128,128]{3,0,2,1:T(8,128)S(1)}, u32[]{:S(2)}) copy-start(f32[16,2,128,128]{3,0,2,1:T(8,128)S(1)} %fusion.672) | copy-start | bytes 6291460 | tf_op jit(solution)/shard_map/while
  75.6 5.4 copy-start.9
  102.3 8.5 %copy-start.30 = (f32[8,1,128,128]{3,0,2,1:T(8,128)}, f32[8,1,128,128]{3,0,2,1:T(8,128)S(1)}, u32[]{:S(2)}) copy-start(f32[8,1,128,128]{3,0,2,1:T(8,128)S(1)} %get-tuple-element.1574) | copy-start | bytes 1572868 | tf_op jit(solution)/shard_map/while
  105.0 12.2 %copy-start = (f32[16,2,128,128]{3,0,2,1:T(8,128)}, f32[16,2,128,128]{3,0,2,1:T(8,128)S(1)}, u32[]{:S(2)}) copy-start(f32[16,2,128,128]{3,0,2,1:T(8,128)S(1)} %fusion.672) | copy-start | bytes 6291460 | tf_op jit(solution)/shard_map/while
  153.7 5.6 copy-start.9
  187.1 14.3 %copy-start.25 = (f32[3,256,256]{1,2,0:T(8,128)S(1)}, f32[3,256,256]{1,2,0:T(8,128)}, u32[]{:S(2)}) copy-start(f32[3,256,256]{1,2,0:T(8,128)} %get-tuple-element.939) | copy-start | bytes 2359300
  189.5 10.7 %collective-permute-start.5 = (f32[3,64,256]{1,2,0:T(8,128)S(1)}, f32[3,64,256]{1,2,0:T(8,128)S(1)}, u32[]{:S(2)}, u32[]{:S(2)}) collective-permute-start(f32[3,64,256]{1,2,0:T(8,128)S(1)} %get-tuple-element.1300), channel_id=1, source_target_pairs={{8,0},{16,8},{24,16},{9,1},{17,9},{25,17},{10,2},{18,10},{26,18},{... | collective-permute-start | bytes 589832 | tf_op jit(solution)/shard_map/ppermute | solution.py:29
  196.5 4.9 collective-permute-start.4
  200.2 28.4 %copy-start.49 = (f32[2,128,128]{1,2,0:T(8,128)S(1)}, f32[2,128,128]{1,2,0:T(8,128)}, u32[]{:S(2)}) copy-start(f32[2,128,128]{1,2,0:T(8,128)} %copy.121) | copy-start | bytes 393220
  200.2 452.5 %all-reduce.5.cloned.1.call-start = ((), (), s32[]{:S(2)}) async-start(), calls=%async_computation | async-start | bytes 3145728 | tf_op jit(solution)/shard_map/psum | solution.py:184
  201.6 18.0 %collective-permute-start.7 = (f32[3,384,64]{1,2,0:T(8,128)S(1)}, f32[3,384,64]{1,2,0:T(8,128)S(1)}, u32[]{:S(2)}, u32[]{:S(2)}) collective-permute-start(f32[3,384,64]{1,2,0:T(8,128)S(1)} %get-tuple-element.1296), channel_id=1, source_target_pairs={{1,0},{2,1},{3,2},{4,3},{5,4},{6,5},{7,6},{9,8},{10,9},{11,10},{12... | collective-permute-start | bytes 884744 | tf_op jit(solution)/shard_map/ppermute | solution.py:29
  202.9 16.7 %collective-permute-start.6 = (f32[3,384,64]{1,2,0:T(8,128)S(1)}, f32[3,384,64]{1,2,0:T(8,128)S(1)}, u32[]{:S(2)}, u32[]{:S(2)}) collective-permute-start(f32[3,384,64]{1,2,0:T(8,128)S(1)} %get-tuple-element.1297), channel_id=1, source_target_pairs={{0,1},{1,2},{2,3},{3,4},{4,5},{5,6},{6,7},{8,9},{9,10},{10,11},{11... | collective-permute-start | bytes 884744 | tf_op jit(solution)/shard_map/ppermute | solution.py:26
  228.6 19.8 %copy-start.43 = (f32[2,128,128]{1,2,0:T(8,128)}, f32[2,128,128]{1,2,0:T(8,128)S(1)}, u32[]{:S(2)}) copy-start(f32[2,128,128]{1,2,0:T(8,128)S(1)} %fusion.407) | copy-start | bytes 393220
  228.6 115.6 %copy-start.39 = (f32[8,2,128,128]{3,2,1,0:T(8,128)S(1)}, f32[8,2,128,128]{3,2,1,0:T(8,128)}, u32[]{:S(2)}) copy-start(f32[8,2,128,128]{3,2,1,0:T(8,128)} %param.43) | copy-start | bytes 3145732
  228.7 7.1 %collective-permute-start.8 = (f32[2,64,128]{1,2,0:T(8,128)S(1)}, f32[2,64,128]{1,2,0:T(8,128)S(1)}, u32[]{:S(2)}, u32[]{:S(2)}) collective-permute-start(f32[2,64,128]{1,2,0:T(8,128)S(1)} %get-tuple-element.1306), channel_id=1, source_target_pairs={{0,8},{8,16},{16,24},{1,9},{9,17},{17,25},{2,10},{10,18},{18,26},{... | collective-permute-start | bytes 196616 | tf_op jit(solution)/shard_map/ppermute | solution.py:26
  230.2 6.6 collective-permute-start.9
  237.0 6.0 collective-permute-start.10
  241.1 7.3 %collective-permute-start.11 = (f32[2,256,64]{1,2,0:T(8,128)S(1)}, f32[2,256,64]{1,2,0:T(8,128)S(1)}, u32[]{:S(2)}, u32[]{:S(2)}) collective-permute-start(f32[2,256,64]{1,2,0:T(8,128)S(1)} %get-tuple-element.1303), channel_id=1, source_target_pairs={{1,0},{2,1},{3,2},{4,3},{5,4},{6,5},{7,6},{9,8},{10,9},{11,10},{12... | collective-permute-start | bytes 393224 | tf_op jit(solution)/shard_map/ppermute | solution.py:29
  347.0 8.5 %copy-start.32 = (f32[8,1,128,128]{3,0,2,1:T(8,128)}, f32[8,1,128,128]{3,0,2,1:T(8,128)S(1)}, u32[]{:S(2)}) copy-start(f32[8,1,128,128]{3,0,2,1:T(8,128)S(1)} %get-tuple-element.1625) | copy-start | bytes 1572868 | tf_op jit(solution)/shard_map/while
  349.8 11.2 %copy-start.2 = (f32[16,2,128,128]{3,0,2,1:T(8,128)}, f32[16,2,128,128]{3,0,2,1:T(8,128)S(1)}, u32[]{:S(2)}) copy-start(f32[16,2,128,128]{3,0,2,1:T(8,128)S(1)} %fusion.747) | copy-start | bytes 6291460 | tf_op jit(solution)/shard_map/while
  373.6 5.9 copy-start.54
  397.7 5.4 copy-start.11
  424.5 8.5 %copy-start.32 = (f32[8,1,128,128]{3,0,2,1:T(8,128)}, f32[8,1,128,128]{3,0,2,1:T(8,128)S(1)}, u32[]{:S(2)}) copy-start(f32[8,1,128,128]{3,0,2,1:T(8,128)S(1)} %get-tuple-element.1625) | copy-start | bytes 1572868 | tf_op jit(solution)/shard_map/while
  427.3 12.2 %copy-start.2 = (f32[16,2,128,128]{3,0,2,1:T(8,128)}, f32[16,2,128,128]{3,0,2,1:T(8,128)S(1)}, u32[]{:S(2)}) copy-start(f32[16,2,128,128]{3,0,2,1:T(8,128)S(1)} %fusion.747) | copy-start | bytes 6291460 | tf_op jit(solution)/shard_map/while
  452.0 5.9 copy-start.54
  476.0 5.6 copy-start.11
  508.2 11.6 %copy-start.51 = (f32[32,8]{0,1:T(8,128)}, f32[32,8]{0,1:T(8,128)S(1)}, u32[]{:S(2)}) copy-start(f32[32,8]{0,1:T(8,128)S(1)} %get-tuple-element.948) | copy-start | bytes 3076
  508.2 9.5 %copy-start.36 = (f32[8,128,128]{2,0,1:T(8,128)S(1)}, f32[8,128,128]{2,0,1:T(8,128)}, u32[]{:S(2)}) copy-start(f32[8,128,128]{2,0,1:T(8,128)} %get-tuple-element.946) | copy-start | bytes 1572868
  508.3 10.4 %copy-start.22 = (f32[3,256,256]{1,2,0:T(8,128)S(1)}, f32[3,256,256]{1,2,0:T(8,128)}, u32[]{:S(2)}) copy-start(f32[3,256,256]{1,2,0:T(8,128)} %get-tuple-element.944) | copy-start | bytes 2359300
  509.6 9.0 %collective-permute-start.13 = (f32[3,64,256]{1,2,0:T(8,128)S(1)}, f32[3,64,256]{1,2,0:T(8,128)S(1)}, u32[]{:S(2)}, u32[]{:S(2)}) collective-permute-start(f32[3,64,256]{1,2,0:T(8,128)S(1)} %get-tuple-element.1298), channel_id=1, source_target_pairs={{8,0},{16,8},{24,16},{9,1},{17,9},{25,17},{10,2},{18,10},{26,18},{... | collective-permute-start | bytes 589832 | tf_op jit(solution)/shard_map/ppermute | solution.py:29
  513.3 5.3 collective-permute-start.12
  518.6 35.0 %copy-start.44 = (f32[2,128,128]{1,2,0:T(8,128)S(1)}, f32[2,128,128]{1,2,0:T(8,128)}, u32[]{:S(2)}) copy-start(f32[2,128,128]{1,2,0:T(8,128)} %copy-done.43) | copy-start | bytes 393220
  519.8 20.5 %collective-permute-start.15 = (f32[3,384,64]{1,2,0:T(8,128)}, f32[3,384,64]{1,2,0:T(8,128)}, u32[]{:S(2)}, u32[]{:S(2)}) collective-permute-start(f32[3,384,64]{1,2,0:T(8,128)} %get-tuple-element.1294), channel_id=1, source_target_pairs={{1,0},{2,1},{3,2},{4,3},{5,4},{6,5},{7,6},{9,8},{10,9},{11,10},{12... | collective-permute-start | bytes 884744 | tf_op jit(solution)/shard_map/ppermute | solution.py:29
  521.1 18.3 %collective-permute-start.14 = (f32[3,384,64]{1,2,0:T(8,128)}, f32[3,384,64]{1,2,0:T(8,128)}, u32[]{:S(2)}, u32[]{:S(2)}) collective-permute-start(f32[3,384,64]{1,2,0:T(8,128)} %get-tuple-element.1295), channel_id=1, source_target_pairs={{0,1},{1,2},{2,3},{3,4},{4,5},{5,6},{6,7},{8,9},{9,10},{10,11},{11... | collective-permute-start | bytes 884744 | tf_op jit(solution)/shard_map/ppermute | solution.py:26
  526.4 127.5 %copy-start.40 = (f32[8,2,128,128]{3,2,1,0:T(8,128)S(1)}, f32[8,2,128,128]{3,2,1,0:T(8,128)}, u32[]{:S(2)}) copy-start(f32[8,2,128,128]{3,2,1,0:T(8,128)} %param.43) | copy-start | bytes 3145732
  526.4 127.5 %copy-start.42 = (f32[8,128,128]{2,1,0:T(8,128)S(1)}, f32[8,128,128]{2,1,0:T(8,128)}, u32[]{:S(2)}) copy-start(f32[8,128,128]{2,1,0:T(8,128)} %copy-done.41) | copy-start | bytes 1572868
  526.4 127.5 %copy-start.46 = (f32[8,1,128,128]{3,2,1,0:T(8,128)S(1)}, f32[8,1,128,128]{3,2,1,0:T(8,128)}, u32[]{:S(2)}) copy-start(f32[8,1,128,128]{3,2,1,0:T(8,128)} %get-tuple-element.1259) | copy-start | bytes 1572868
  526.4 127.5 %copy-start.47 = (f32[8,1,128,128]{3,2,1,0:T(8,128)S(1)}, f32[8,1,128,128]{3,2,1,0:T(8,128)}, u32[]{:S(2)}) copy-start(f32[8,1,128,128]{3,2,1,0:T(8,128)} %get-tuple-element.1260) | copy-start | bytes 1572868
  (63 other events, 198.7 us)
Sparse Core Ops, SparseCore 0:
  200.3 142.6 all-reduce.6
  518.8 133.9 all-reduce.4
where the time goes:
time: 671 us; the launch traced here: 664 us
  matrix products  249 us (37%)
  waiting for transfers between devices  226 us (34%)
  local copies, waits for them, and re-layouts  75.5 us (11%)
  starting transfers between devices  45.9 us (7%)
  other arithmetic  38.4 us (6%)
  between operations  15.2 us (2%)
  loops' own time  13.2 us (2%)
    psum x2, waiting for transfers between devices, shards(): totals = lax.psum((moment_real, moment_imag, moment_power), ('row', 'col'))  193 us
    ppermute x8, starting transfers between devices, extended_2(): lax.ppermute(lax.slice_in_dim(block, 0, width, axis=dim), axis, backward)  24 us
    ppermute x8, waiting for transfers between devices, extended_2(): lax.ppermute(lax.slice_in_dim(block, block.shape[dim] - width, None, axis...  23.7 us
    dot_general x8, matrix products, right_apply(): jnp.einsum('nab,bc->nac', imag_part, cos_part, precision=highest)  22.7 us
    ppermute x8, starting transfers between devices, extended_2(): lax.ppermute(lax.slice_in_dim(block, block.shape[dim] - width, None, axis...  21.8 us
    dot_general x8, matrix products, left_apply(): jnp.einsum('ab,nbc->nac', sin_part, real_part, precision=highest)  21.5 us
    dot_general x8, matrix products, right_apply(): jnp.einsum('nab,bc->nac', real_part, sin_part, precision=highest)  19.2 us
    dot_general x8, matrix products, right_apply(): jnp.einsum('nab,bc->nac', real_part, cos_part, precision=highest)  18.1 us
  transfers between devices with their start and end apart: 18, of which 9 were waited for; matrix products, arithmetic and copies ran while one was open for 6% of the time, Pallas kernels for 0%

commit v1 on v0

v1 whole, which is shorter than its diff:
```python
import functools
import math

import jax
import jax.numpy as jnp
import numpy as np
from jax import lax
from jax.experimental import pallas as pl
from jax.experimental.pallas import tpu as pltpu
from jax.sharding import PartitionSpec as P

ITERS = 2
GROUP = 4
VMEM_LIMIT = 48 * 1024 * 1024

amp_floor = 0.5
count_scale = 0.03125


def extended_2(block, sides, width):
    for axis, dim in sides:
        count = lax.axis_size(axis)
        forward = [(i, i + 1) for i in range(count - 1)]
        backward = [(target, source) for source, target in forward]
        low = lax.ppermute(
            lax.slice_in_dim(block, block.shape[dim] - width, None, axis=dim), axis, forward
        )
        high = lax.ppermute(lax.slice_in_dim(block, 0, width, axis=dim), axis, backward)
        block = jnp.concatenate([low, block, high], axis=dim)
    return block


def halves(values):
    high = values.astype(jnp.bfloat16)
    low = (values - high.astype(jnp.float32)).astype(jnp.bfloat16)
    return high, low


def dft_tables(length):
    ramp = np.arange(length)
    angles = (ramp[:, None] * ramp[None, :] % length) * (2.0 * math.pi / length)
    cos = np.cos(angles) / math.sqrt(length)
    sin = -np.sin(angles) / math.sqrt(length)
    tables = []
    for part in (sin, -sin):
        right = jnp.asarray(np.block([[cos, part], [-part, cos]]), jnp.float32)
        left = jnp.asarray(np.block([[cos, -part], [part, cos]]), jnp.float32)
        high, low = halves(right)
        tables.append(jnp.concatenate([high, low, high], axis=0))
        high, low = halves(left)
        tables.append(jnp.concatenate([high, low, high], axis=1))
    return tables


def right_apply(values, table):
    high, low = halves(values)
    return jnp.dot(
        jnp.concatenate([high, high, low], axis=1), table, preferred_element_type=jnp.float32
    )


def left_apply(table, values):
    high, low = halves(values)
    return jnp.dot(
        table, jnp.concatenate([high, high, low], axis=0), preferred_element_type=jnp.float32
    )


def positions_kernel(
    count_ref, offs_ref, coef_ref, ext_ref, modes_ref, photon_ref, fr_ref, fl_ref, br_ref, bl_ref,
    acc_ref, mom_ref, num_ref, den_ref, obj_s, prb_s, psi_s, cross_s, power_s,
):
    modes, _, size, _ = modes_ref.shape
    extent = 2 * size
    step = 16
    chunks = size // step
    acc_ref[...] = jnp.zeros_like(acc_ref)
    mom_ref[...] = jnp.zeros_like(mom_ref)
    num_ref[...] = jnp.zeros_like(num_ref)
    den_ref[...] = jnp.zeros_like(den_ref)
    for k in range(modes):
        re, im = modes_ref[k, 0], modes_ref[k, 1]
        power_s[k] = re * re + im * im
    lane = lax.broadcasted_iota(jnp.int32, (size, size), 1)
    live = count_ref[0]

    def group(number, carry):
        first = number * GROUP
        weights = [[coef_ref[first + g, k] for k in range(modes)] for g in range(GROUP)]
        gates = [jnp.where(first + g < live, 1.0, 0.0).astype(jnp.float32) for g in range(GROUP)]
        corners = [(offs_ref[first + g, 0], offs_ref[first + g, 1]) for g in range(GROUP)]

        def probe_rows(chunk, carry):
            rows = pl.ds(pl.multiple_of(chunk * 8, 8), 8)
            for comp in range(2):
                parts = [modes_ref[k, comp, rows, :] for k in range(modes)]
                for g in range(GROUP):
                    total = weights[g][0] * parts[0]
                    for k in range(1, modes):
                        total = total + weights[g][k] * parts[k]
                    prb_s[g, comp, rows, :] = total
            return carry

        lax.fori_loop(0, size // 8, probe_rows, 0, unroll=2)

        for g in range(GROUP):
            top, left = corners[g]
            for comp in range(2):
                low = ext_ref[pl.ds(2 * comp * extent + top, size), :]
                high = ext_ref[pl.ds((2 * comp + 1) * extent + top, size), :]
                picked = jnp.where(lane >= left, low, high)
                obj_s[g, comp] = pltpu.roll(picked, lax.rem(size - left, size), 1)
            pr, pi, ore, oim = prb_s[g, 0], prb_s[g, 1], obj_s[g, 0], obj_s[g, 1]
            psi_s[g, :, :size] = pr * ore - pi * oim
            psi_s[g, :, size:] = pr * oim + pi * ore

        rowed = right_apply(psi_s[...].reshape(GROUP * size, 2 * size), fr_ref[...])
        for pair in range(GROUP // 2):
            one = rowed[2 * pair * size : (2 * pair + 1) * size]
            two = rowed[(2 * pair + 1) * size : (2 * pair + 2) * size]
            stacked = jnp.concatenate(
                [
                    jnp.concatenate([one[:, :size], two[:, :size]], axis=1),
                    jnp.concatenate([one[:, size:], two[:, size:]], axis=1),
                ],
                axis=0,
            )
            far = left_apply(fl_ref[...], stacked)
            far_real, far_imag = far[:size], far[size:]
            photons = jnp.concatenate(
                [photon_ref[first + 2 * pair], photon_ref[first + 2 * pair + 1]], axis=1
            )
            target = jnp.sqrt(photons.astype(jnp.float32)) * count_scale
            square = far_real * far_real + far_imag * far_imag
            scaling = target * lax.rsqrt(jnp.maximum(square, amp_floor * amp_floor))
            fixed = jnp.concatenate([far_real * scaling, far_imag * scaling], axis=0)
            near = left_apply(bl_ref[...], fixed)
            for half in range(2):
                g = 2 * pair + half
                cols = slice(half * size, (half + 1) * size)
                mixed = jnp.concatenate([near[:size, cols], near[size:, cols]], axis=1)
                back = right_apply(mixed, br_ref[...])
                diff = (back - psi_s[g]) * gates[g]
                dr, di = diff[:, :size], diff[:, size:]
                pr, pi, ore, oim = prb_s[g, 0], prb_s[g, 1], obj_s[g, 0], obj_s[g, 1]
                cross_s[g, 0] = ore * dr + oim * di
                cross_s[g, 1] = ore * di - oim * dr
                cross_s[g, 2] = (ore * ore + oim * oim) * gates[g]
                top, left = corners[g]
                pieces = (
                    pr * dr + pi * di,
                    pr * di - pi * dr,
                    (pr * pr + pi * pi) * gates[g],
                )
                inside = lane >= left
                for comp in range(3):
                    moved = pltpu.roll(pieces[comp], lax.rem(left, size), 1)
                    low = pl.ds(2 * comp * extent + top, size)
                    high = pl.ds((2 * comp + 1) * extent + top, size)
                    acc_ref[low, :] += jnp.where(inside, moved, 0.0)
                    acc_ref[high, :] += jnp.where(inside, 0.0, moved)

        def mode_sums(k, carry):
            used = [coef_ref[first + g, k] for g in range(GROUP)]

            def rows_sums(chunk, sums):
                rows = pl.ds(pl.multiple_of(chunk * step, step), step)
                re, im, power = modes_ref[k, 0, rows, :], modes_ref[k, 1, rows, :], power_s[k, rows, :]
                totals = [mom_ref[c, k, rows, :] for c in range(3)]
                new = []
                for g in range(GROUP):
                    cr, ci, cp = (cross_s[g, c, rows, :] for c in range(3))
                    totals[0] = totals[0] + used[g] * cr
                    totals[1] = totals[1] + used[g] * ci
                    totals[2] = totals[2] + (used[g] * used[g]) * cp
                    num = (cr * re + ci * im).reshape(step // 8, 8, size).sum(axis=0)
                    den = (cp * power).reshape(step // 8, 8, size).sum(axis=0)
                    new.append((sums[g][0] + num, sums[g][1] + den))
                for c in range(3):
                    mom_ref[c, k, rows, :] = totals[c]
                return tuple(new)

            zero = jnp.zeros((8, size), jnp.float32)
            sums = lax.fori_loop(
                0, chunks, rows_sums, tuple((zero, zero) for _ in range(GROUP)), unroll=4
            )
            for g in range(GROUP):
                num_ref[first + g, pl.ds(k, 1), :] = sums[g][0].sum(axis=0, keepdims=True)
                den_ref[first + g, pl.ds(k, 1), :] = sums[g][1].sum(axis=0, keepdims=True)
            return carry

        lax.fori_loop(0, modes, mode_sums, 0)
        return carry

    lax.fori_loop(0, (live + GROUP - 1) // GROUP, group, 0)


def positions_call(count, offs, coef, ext, modes, photons, tables):
    slots, kinds = coef.shape
    size = modes.shape[-1]
    extent = 2 * size
    smem = pl.BlockSpec(memory_space=pltpu.SMEM)
    vmem = pl.BlockSpec(memory_space=pltpu.VMEM)
    f32 = jnp.float32
    return pl.pallas_call(
        positions_kernel,
        out_shape=(
            jax.ShapeDtypeStruct((6 * extent, size), f32),
            jax.ShapeDtypeStruct((3, kinds, size, size), f32),
            jax.ShapeDtypeStruct((slots, kinds, size), f32),
            jax.ShapeDtypeStruct((slots, kinds, size), f32),
        ),
        in_specs=[smem] * 3 + [vmem] * 7,
        out_specs=(vmem,) * 4,
        scratch_shapes=[
            pltpu.VMEM((GROUP, 2, size, size), f32),
            pltpu.VMEM((GROUP, 2, size, size), f32),
            pltpu.VMEM((GROUP, size, 2 * size), f32),
            pltpu.VMEM((GROUP, 3, size, size), f32),
            pltpu.VMEM((kinds, size, size), f32),
        ],
        compiler_params=pltpu.CompilerParams(vmem_limit_bytes=VMEM_LIMIT),
        name="positions",
    )(count, offs, coef, ext, modes, photons, *tables)


def fold_edges(padded, margin):
    tile_width = padded.shape[1] - 4 * margin
    lower_edge = 2 * margin
    upper_edge = tile_width + 2 * margin
    outer_edge = tile_width + 3 * margin
    inner_end = tile_width - margin
    interior = padded[:, lower_edge:upper_edge, lower_edge:upper_edge]
    interior = interior.at[:, :margin, :].add(padded[:, :margin, lower_edge:upper_edge])
    interior = interior.at[:, inner_end:, :].add(padded[:, outer_edge:, lower_edge:upper_edge])
    interior = interior.at[:, :, :margin].add(padded[:, lower_edge:upper_edge, :margin])
    interior = interior.at[:, :, inner_end:].add(padded[:, lower_edge:upper_edge, outer_edge:])
    interior = interior.at[:, :margin, :margin].add(padded[:, :margin, :margin])
    interior = interior.at[:, :margin, inner_end:].add(padded[:, :margin, outer_edge:])
    interior = interior.at[:, inner_end:, :margin].add(padded[:, outer_edge:, :margin])
    interior = interior.at[:, inner_end:, inner_end:].add(padded[:, outer_edge:, outer_edge:])
    return interior


def folded(block, sides, width):
    for axis, dim in sides:
        count = lax.axis_size(axis)
        forward = [(i, i + 1) for i in range(count - 1)]
        backward = [(target, source) for source, target in forward]
        size = block.shape[dim] - 2 * width
        low = lax.ppermute(lax.slice_in_dim(block, 0, width, axis=dim), axis, backward)
        high = lax.ppermute(lax.slice_in_dim(block, size + width, None, axis=dim), axis, forward)
        inner = lax.slice_in_dim(block, width, size + width, axis=dim)
        first = lax.slice_in_dim(inner, 0, width, axis=dim) + high
        last = lax.slice_in_dim(inner, size - width, None, axis=dim) + low
        middle = lax.slice_in_dim(inner, width, size - width, axis=dim)
        block = jnp.concatenate([first, middle, last], axis=dim)
    return block


def shards(object_field, probe_modes, coefficients, offsets, counts, measured):
    size = measured.shape[-1]
    margin = size // 2
    extent = object_field.shape[1] + size
    tables = dft_tables(size)
    coef = coefficients[0, 0]
    sides = (("row", 1), ("col", 2))
    for iteration in range(ITERS):
        extended = extended_2(object_field, sides, margin)
        ext = extended.reshape(2, extent, 2, size).transpose(0, 2, 1, 3).reshape(-1, size)
        acc, moments, num, den = positions_call(
            counts[0], offsets[0, 0], coef, ext, probe_modes, measured[0, 0], tables
        )
        coef = coef + num.sum(axis=-1) / (den.sum(axis=-1) + 1.0)
        acc = acc.reshape(3, 2, extent, size).transpose(0, 2, 1, 3).reshape(3, extent, extent)
        interior = folded(acc, sides, margin)
        object_field = object_field + interior[0:2] / (interior[2:3] + 1.0)
        totals = lax.psum(moments, ("row", "col"))
        probe_modes = probe_modes + jnp.stack([totals[0], totals[1]], axis=1) / (
            totals[2][:, None] + 1.0
        )
    return (object_field, probe_modes, coef[None, None])


def solution(mesh):
    placed = (
        P(None, "row", "col"),
        P(),
        P("row", "col", None, None),
        P("row", "col", None, None),
        P("row", "col"),
        P("row", "col", None, None, None),
    )
    return jax.shard_map(
        shards,
        mesh=mesh,
        in_specs=placed,
        out_specs=(P(None, "row", "col"), P(), P("row", "col", None, None)),
        check_vma=False,
    )
```

time: 671 us -> 408 us (0.61)
  matrix products: 249 us -> 0 us
  local copies, waits for them, and re-layouts: 75.5 us -> 6.04 us
  waiting for transfers between devices: 226 us -> 280 us
  Pallas kernels: 0 us -> 43.6 us
  other arithmetic: 38.4 us -> 7.01 us
  loops' own time: 13.2 us -> 0 us
    dot_general x108 -> x0, matrix products: 249 us -> none  [the longest x8 22.7 us: right_apply(): jnp.einsum('nab,bc->nac', imag_part, cos_part, precision=highest)]
    pallas_call x0 -> x2, Pallas kernels: none -> 43.6 us  [positions_call(): pl.pallas_call(positions_kernel, out_shape=(jax.ShapeDtypeStruct((6 * ext...]
    ppermute x0 -> x8, waiting for transfers between devices: none -> 36.3 us  [the longest x4 31.6 us: folded(): lax.ppermute(lax.slice_in_dim(block, size + width, None, axis=dim), axis,...]
    ppermute x0 -> x8, starting transfers between devices: none -> 27.7 us  [the longest x4 16.6 us: folded(): lax.ppermute(lax.slice_in_dim(block, 0, width, axis=dim), axis, backward)]
    psum x2, waiting for transfers between devices: 193 us -> 220 us  [shards(): totals = lax.psum(moments, ('row', 'col'))]
    scatter-add x12 -> x0, local copies, waits for them, and re-layouts: 16.1 us -> none  [the longest x2 4.02 us: fold_edges(): interior.at[:, :margin, inner_end:].add(padded[:, :margin, outer_edge:])]
    sub x8 -> x0, local copies, waits for them, and re-layouts: 16.1 us -> none  [the longest x4 10.5 us: left_apply(): jnp.einsum('ab,nbc->nac', cos_part, real_part, precision=highest)]
    add x22 -> x10, other arithmetic: 17.8 us -> 1.79 us  [the longest x2 1.4 us: shards(): probe_modes + jnp.stack([totals[0], totals[1]], axis=1) / (totals[2][:, N...]
  transfers between devices with their start and end apart: 18 -> 18, of which waited for: 9 -> 15; matrix products, arithmetic and copies ran while one was open for 6% -> 1% of each run, Pallas kernels for 0% -> 0%
where the time goes in v1:
time: 408 us; the launch traced here: 403 us
  waiting for transfers between devices  280 us (69%)
  starting transfers between devices  51.9 us (13%)
  Pallas kernels  43.6 us (11%)
  between operations  15.3 us (4%)
  other arithmetic  7.01 us (2%)
  local copies, waits for them, and re-layouts  6.04 us (1%)
    psum x2, waiting for transfers between devices, shards(): totals = lax.psum(moments, ('row', 'col'))  220 us
    pallas_call x2, Pallas kernels, positions_call(): pl.pallas_call(positions_kernel, out_shape=(jax.ShapeDtypeStruct((6 * ext...  43.6 us
    ppermute x4, waiting for transfers between devices, folded(): lax.ppermute(lax.slice_in_dim(block, size + width, None, axis=dim), axis,...  31.6 us
    ppermute x4, waiting for transfers between devices, extended_2(): lax.ppermute(lax.slice_in_dim(block, block.shape[dim] - width, None, axis...  19.4 us
    ppermute x4, starting transfers between devices, folded(): lax.ppermute(lax.slice_in_dim(block, 0, width, axis=dim), axis, backward)  16.6 us
    ppermute x4, starting transfers between devices, extended_2(): lax.ppermute(lax.slice_in_dim(block, 0, width, axis=dim), axis, backward)  12.9 us
    ppermute x4, starting transfers between devices, extended_2(): lax.ppermute(lax.slice_in_dim(block, block.shape[dim] - width, None, axis...  11.3 us
    ppermute x4, starting transfers between devices, folded(): lax.ppermute(lax.slice_in_dim(block, size + width, None, axis=dim), axis,...  11.1 us
  transfers between devices with their start and end apart: 18, of which 15 were waited for; matrix products, arithmetic and copies ran while one was open for 1% of the time, Pallas kernels for 0%

profile of v1, /device:TPU:5, one launch (start us, length us, event | category | flops | bytes accessed | tf_op | source)
XLA Modules:
  0.0 403.4 jit_solution(6605623598138361137)
XLA Ops:
  7.3 1.0 fusion.26
  8.3 1.3 collective-permute-start
  9.6 3.2 collective-permute-start.1
  12.9 0.9 constant_dynamic-update-slice_fusion.1
  13.8 0.9 fusion.24
  14.7 1.3 collective-permute-start.3
  16.0 4.0 collective-permute-start.2
  20.8 1.2 collective-permute-done.3
  22.0 8.3 %collective-permute-done.2 = f32[2,256,64]{2,1,0:T(8,128)S(1)} collective-permute-done((f32[2,256,64]{2,1,0:T(8,128)}, f32[2,256,64]{2,1,0:T(8,128)S(1)}, u32[]{:S(2)}, u32[]{:S(2)}) %collective-permute-start.2) | collective-permute-done | bytes 131104 | tf_op jit(solution)/shard_map/ppermute | solution.py:25
  30.3 0.3 copy_bitcast_fusion.3
  30.6 22.4 %positions.2 = (f32[1536,128]{1,0:T(8,128)S(1)}, f32[3,8,128,128]{3,2,1,0:T(8,128)}, f32[32,8,128]{2,1,0:T(8,128)S(1)}, f32[32,8,128]{2,1,0:T(8,128)S(1)}) custom-call(s32[1]{0:T(128)} %bitcast.59.count_ref, s32[32,2]{1,0:T(8,128)S(1)} %copy.15.offs_ref, f32[32,8]{1,0:T(8,128)S(1)} %bitcast.65, f32[1024,128]{1,0:T(8,128)S(1)} %bitcast.62, ...), custom_call_target="tpu_custom_call" | custom-call | tf_op jit(solution)/shard_map/positions/pallas_call | solution.py:205
  53.1 6.6 %collective-permute-start.5 = (f32[3,64,256]{2,1,0:T(8,128)S(1)}, f32[3,64,256]{2,1,0:T(8,128)S(1)}, u32[]{:S(2)}, u32[]{:S(2)}) collective-permute-start(f32[3,64,256]{2,1,0:T(8,128)S(1)} %slice.153), channel_id=1, source_target_pairs={{8,0},{16,8},{24,16},{9,1},{17,9},{25,17},{10,2},{18,10},{26,18},{... | collective-permute-start | bytes 589832 | tf_op jit(solution)/shard_map/ppermute | solution.py:251
  59.7 1.0 collective-permute-done.5
  60.8 1.3 collective-permute-start.4
  62.1 13.5 %collective-permute-done.4 = f32[3,64,256]{2,1,0:T(8,128)S(1)} collective-permute-done((f32[3,64,256]{2,1,0:T(8,128)S(1)}, f32[3,64,256]{2,1,0:T(8,128)S(1)}, u32[]{:S(2)}, u32[]{:S(2)}) %collective-permute-start.4) | collective-permute-done | bytes 196640 | tf_op jit(solution)/shard_map/ppermute | solution.py:252
  75.7 1.3 collective-permute-start.7
  77.0 4.5 %collective-permute-start.6 = (f32[3,128,64]{2,1,0:T(8,128)S(1)}, f32[3,128,64]{2,1,0:T(8,128)S(1)}, u32[]{:S(2)}, u32[]{:S(2)}) collective-permute-start(f32[3,128,64]{2,1,0:T(8,128)S(1)} %get-tuple-element.39), channel_id=1, source_target_pairs={{0,1},{1,2},{2,3},{3,4},{4,5},{5,6},{6,7},{8,9},{9,10},{10,11},{11... | collective-permute-start | bytes 294920 | tf_op jit(solution)/shard_map/ppermute | solution.py:252
  81.7 1.0 collective-permute-done.7
  82.7 2.6 collective-permute-done.6
  85.6 7.1 %collective-permute-start.9 = (f32[2,64,128]{2,1,0:T(8,128)S(1)}, f32[2,64,128]{2,1,0:T(8,128)S(1)}, u32[]{:S(2)}, u32[]{:S(2)}) collective-permute-start(f32[2,64,128]{2,1,0:T(8,128)S(1)} %get-tuple-element.45), channel_id=1, source_target_pairs={{8,0},{16,8},{24,16},{9,1},{17,9},{25,17},{10,2},{18,10},{26,18},{... | collective-permute-start | bytes 196616 | tf_op jit(solution)/shard_map/ppermute | solution.py:28
  92.7 1.3 collective-permute-start.8
  94.2 3.2 collective-permute-done.8
  97.5 0.1 fusion.23
  97.6 1.3 collective-permute-start.11
  98.9 4.7 %collective-permute-start.10 = (f32[2,256,64]{2,1,0:T(8,128)S(1)}, f32[2,256,64]{2,1,0:T(8,128)S(1)}, u32[]{:S(2)}, u32[]{:S(2)}) collective-permute-start(f32[2,256,64]{2,1,0:T(8,128)S(1)} %get-tuple-element.40), channel_id=1, source_target_pairs={{0,1},{1,2},{2,3},{3,4},{4,5},{5,6},{6,7},{8,9},{9,10},{10,11},{11... | collective-permute-start | bytes 393224 | tf_op jit(solution)/shard_map/ppermute | solution.py:25
  103.6 3.2 collective-permute-done.11
  106.7 7.9 %collective-permute-done.10 = f32[2,256,64]{2,1,0:T(8,128)S(1)} collective-permute-done((f32[2,256,64]{2,1,0:T(8,128)S(1)}, f32[2,256,64]{2,1,0:T(8,128)S(1)}, u32[]{:S(2)}, u32[]{:S(2)}) %collective-permute-start.10) | collective-permute-done | bytes 131104 | tf_op jit(solution)/shard_map/ppermute | solution.py:25
  114.6 0.3 copy_bitcast_fusion.2
  114.9 104.2 %all-reduce.3.cloned.1.call-done = f32[3,8,128,128]{3,2,1,0:T(8,128)} async-done(((f32[3,8,128,128]{3,2,1,0:T(8,128)}), f32[3,8,128,128]{3,2,1,0:T(8,128)}) %all-reduce.3.cloned.1.call-update) | async-done | bytes 1572880 | tf_op jit(solution)/shard_map/psum | solution.py:278
  219.1 1.5 fusion.2
  220.6 0.2 copy_add_fusion.modes_ref
  220.8 0.8 copy-done.5
  221.6 0.1 copy-done.7
  221.7 21.2 %positions.3 = (f32[1536,128]{1,0:T(8,128)S(1)}, f32[3,8,128,128]{3,2,1,0:T(8,128)S(1)}, f32[32,8,128]{2,1,0:T(8,128)S(1)}, f32[32,8,128]{2,1,0:T(8,128)S(1)}) custom-call(s32[1]{0:T(128)} %bitcast.60.count_ref, s32[32,2]{1,0:T(8,128)S(1)} %copy.15.offs_ref, f32[32,8]{1,0:T(8,128)S(1)} %bitcast_add_fusion.2.coef_ref, f32[1024,128]{1,0:T(8,128)S(1)} %bitcast.61, ...), custom_call_target="tpu_custom_call" | custom-call | tf_op jit(solution)/shard_map/positions/pallas_call | solution.py:205
  242.9 1.1 copy-done.1
  244.2 7.4 %collective-permute-start.13 = (f32[3,64,256]{2,1,0:T(8,128)S(1)}, f32[3,64,256]{2,1,0:T(8,128)S(1)}, u32[]{:S(2)}, u32[]{:S(2)}) collective-permute-start(f32[3,64,256]{2,1,0:T(8,128)S(1)} %slice.172), channel_id=1, source_target_pairs={{8,0},{16,8},{24,16},{9,1},{17,9},{25,17},{10,2},{18,10},{26,18},{... | collective-permute-start | bytes 589832 | tf_op jit(solution)/shard_map/ppermute | solution.py:251
  251.6 1.0 collective-permute-done.13
  252.7 1.3 collective-permute-start.12
  254.3 10.2 %collective-permute-done.12 = f32[3,64,256]{2,1,0:T(8,128)S(1)} collective-permute-done((f32[3,64,256]{2,1,0:T(8,128)S(1)}, f32[3,64,256]{2,1,0:T(8,128)S(1)}, u32[]{:S(2)}, u32[]{:S(2)}) %collective-permute-start.12) | collective-permute-done | bytes 196640 | tf_op jit(solution)/shard_map/ppermute | solution.py:252
  264.6 1.3 collective-permute-start.15
  265.9 4.0 collective-permute-start.14
  270.0 0.7 copy.23
  270.6 1.6 collective-permute-done.15
  272.2 5.3 %collective-permute-done.14 = f32[3,128,64]{2,1,0:T(8,128)S(1)} collective-permute-done((f32[3,128,64]{2,1,0:T(8,128)S(1)}, f32[3,128,64]{2,1,0:T(8,128)S(1)}, u32[]{:S(2)}, u32[]{:S(2)}) %collective-permute-start.14) | collective-permute-done | bytes 98336 | tf_op jit(solution)/shard_map/ppermute | solution.py:252
  277.7 0.8 fusion.15
  278.5 115.4 %all-reduce.5.cloned.1.call-done = f32[3,8,128,128]{3,2,1,0:T(8,128)} async-done(((f32[3,8,128,128]{3,2,1,0:T(8,128)}), f32[3,8,128,128]{3,2,1,0:T(8,128)}) %all-reduce.5.cloned.1.call-update) | async-done | bytes 1572880 | tf_op jit(solution)/shard_map/psum | solution.py:278
  393.9 1.5 fusion.1
  395.4 1.2 fusion
  (65 shorter events, 1.9 us)
Async XLA Ops:
  7.2 23.4 %copy-start.2 = (bf16[768,256]{1,0:T(8,128)(2,1)S(1)}, bf16[768,256]{1,0:T(8,128)(2,1)}, u32[]{:S(2)}) copy-start(bf16[768,256]{1,0:T(8,128)(2,1)} %constant.20.fr_ref) | copy-start | bytes 1179652
  7.2 23.4 %copy-start.3 = (bf16[256,768]{1,0:T(8,128)(2,1)S(1)}, bf16[256,768]{1,0:T(8,128)(2,1)}, u32[]{:S(2)}) copy-start(bf16[256,768]{1,0:T(8,128)(2,1)} %constant.25.fl_ref) | copy-start | bytes 1179652
  7.2 23.4 %copy-start.4 = (bf16[768,256]{1,0:T(8,128)(2,1)S(1)}, bf16[768,256]{1,0:T(8,128)(2,1)}, u32[]{:S(2)}) copy-start(bf16[768,256]{1,0:T(8,128)(2,1)} %constant.26.br_ref) | copy-start | bytes 1179652
  7.2 23.4 %copy-start.6 = (bf16[256,768]{1,0:T(8,128)(2,1)S(1)}, bf16[256,768]{1,0:T(8,128)(2,1)}, u32[]{:S(2)}) copy-start(bf16[256,768]{1,0:T(8,128)(2,1)} %constant.27.bl_ref) | copy-start | bytes 1179652
  7.2 13.4 %copy-start.16 = (s32[1,1,32,2]{2,3,1,0:T(2,128)S(1)}, s32[1,1,32,2]{2,3,1,0:T(2,128)}, u32[]{:S(2)}) copy-start(s32[1,1,32,2]{2,3,1,0:T(2,128)} %param.13) | copy-start | bytes 772
  7.2 13.5 %copy-start.15 = (f32[1,1,32,8]{2,3,1,0:T(8,128)S(1)}, f32[1,1,32,8]{2,3,1,0:T(8,128)}, u32[]{:S(2)}) copy-start(f32[1,1,32,8]{2,3,1,0:T(8,128)} %param.12) | copy-start | bytes 3076
  7.2 23.4 %copy-start = (f32[8,2,128,128]{3,2,1,0:T(8,128)S(1)}, f32[8,2,128,128]{3,2,1,0:T(8,128)}, u32[]{:S(2)}) copy-start(f32[8,2,128,128]{3,2,1,0:T(8,128)} %modes_ref.1) | copy-start | bytes 3145732
  7.2 211.8 %all-reduce.3.cloned.1.call-start = ((), (), s32[]{:S(2)}) async-start(), calls=%async_computation | async-start | bytes 3145728 | tf_op jit(solution)/shard_map/psum | solution.py:278
  8.3 4.5 %collective-permute-start = (f32[2,64,128]{2,1,0:T(8,128)S(1)}, f32[2,64,128]{2,1,0:T(8,128)S(1)}, u32[]{:S(2)}, u32[]{:S(2)}) collective-permute-start(f32[2,64,128]{2,1,0:T(8,128)S(1)} %get-tuple-element.47), channel_id=1, source_target_pairs={{0,8},{8,16},{16,24},{1,9},{9,17},{17,25},{2,10},{10,18},{18,26},{... | collective-permute-start | bytes 196616 | tf_op jit(solution)/shard_map/ppermute | solution.py:25
  9.6 4.2 %collective-permute-start.1 = (f32[2,64,128]{2,1,0:T(8,128)S(1)}, f32[2,64,128]{2,1,0:T(8,128)S(1)}, u32[]{:S(2)}, u32[]{:S(2)}) collective-permute-start(f32[2,64,128]{2,1,0:T(8,128)S(1)} %get-tuple-element.46), channel_id=1, source_target_pairs={{8,0},{16,8},{24,16},{9,1},{17,9},{25,17},{10,2},{18,10},{26,18},{... | collective-permute-start | bytes 196616 | tf_op jit(solution)/shard_map/ppermute | solution.py:28
  14.7 7.3 %collective-permute-start.3 = (f32[2,256,64]{2,1,0:T(8,128)}, f32[2,256,64]{2,1,0:T(8,128)S(1)}, u32[]{:S(2)}, u32[]{:S(2)}) collective-permute-start(f32[2,256,64]{2,1,0:T(8,128)} %get-tuple-element.43), channel_id=1, source_target_pairs={{1,0},{2,1},{3,2},{4,3},{5,4},{6,5},{7,6},{9,8},{10,9},{11,10},{12... | collective-permute-start | bytes 393224 | tf_op jit(solution)/shard_map/ppermute | solution.py:28
  16.0 14.3 %collective-permute-start.2 = (f32[2,256,64]{2,1,0:T(8,128)}, f32[2,256,64]{2,1,0:T(8,128)S(1)}, u32[]{:S(2)}, u32[]{:S(2)}) collective-permute-start(f32[2,256,64]{2,1,0:T(8,128)} %get-tuple-element.42), channel_id=1, source_target_pairs={{0,1},{1,2},{2,3},{3,4},{4,5},{5,6},{6,7},{8,9},{9,10},{10,11},{11... | collective-permute-start | bytes 393224 | tf_op jit(solution)/shard_map/ppermute | solution.py:25
  53.0 22.6 %copy-start.8 = (f32[32,8,128]{2,1,0:T(8,128)}, f32[32,8,128]{2,1,0:T(8,128)S(1)}, u32[]{:S(2)}) copy-start(f32[32,8,128]{2,1,0:T(8,128)S(1)} %get-tuple-element.13) | copy-start | bytes 393220
  53.0 22.6 %copy-start.10 = (f32[32,8,128]{2,1,0:T(8,128)}, f32[32,8,128]{2,1,0:T(8,128)S(1)}, u32[]{:S(2)}) copy-start(f32[32,8,128]{2,1,0:T(8,128)S(1)} %get-tuple-element.12) | copy-start | bytes 393220
  53.1 7.7 %collective-permute-start.5 = (f32[3,64,256]{2,1,0:T(8,128)S(1)}, f32[3,64,256]{2,1,0:T(8,128)S(1)}, u32[]{:S(2)}, u32[]{:S(2)}) collective-permute-start(f32[3,64,256]{2,1,0:T(8,128)S(1)} %slice.153), channel_id=1, source_target_pairs={{8,0},{16,8},{24,16},{9,1},{17,9},{25,17},{10,2},{18,10},{26,18},{... | collective-permute-start | bytes 589832 | tf_op jit(solution)/shard_map/ppermute | solution.py:251
  60.8 14.8 %collective-permute-start.4 = (f32[3,64,256]{2,1,0:T(8,128)S(1)}, f32[3,64,256]{2,1,0:T(8,128)S(1)}, u32[]{:S(2)}, u32[]{:S(2)}) collective-permute-start(f32[3,64,256]{2,1,0:T(8,128)S(1)} %get-tuple-element.31), channel_id=1, source_target_pairs={{0,8},{8,16},{16,24},{1,9},{9,17},{17,25},{2,10},{10,18},{18,26},{... | collective-permute-start | bytes 589832 | tf_op jit(solution)/shard_map/ppermute | solution.py:252
  75.7 6.9 %collective-permute-start.7 = (f32[3,128,64]{2,1,0:T(8,128)S(1)}, f32[3,128,64]{2,1,0:T(8,128)S(1)}, u32[]{:S(2)}, u32[]{:S(2)}) collective-permute-start(f32[3,128,64]{2,1,0:T(8,128)S(1)} %get-tuple-element.38), channel_id=1, source_target_pairs={{1,0},{2,1},{3,2},{4,3},{5,4},{6,5},{7,6},{9,8},{10,9},{11,10},{12... | collective-permute-start | bytes 294920 | tf_op jit(solution)/shard_map/ppermute | solution.py:251
  77.0 8.2 %collective-permute-start.6 = (f32[3,128,64]{2,1,0:T(8,128)S(1)}, f32[3,128,64]{2,1,0:T(8,128)S(1)}, u32[]{:S(2)}, u32[]{:S(2)}) collective-permute-start(f32[3,128,64]{2,1,0:T(8,128)S(1)} %get-tuple-element.39), channel_id=1, source_target_pairs={{0,1},{1,2},{2,3},{3,4},{4,5},{5,6},{6,7},{8,9},{9,10},{10,11},{11... | collective-permute-start | bytes 294920 | tf_op jit(solution)/shard_map/ppermute | solution.py:252
  81.6 3.9 copy-start.14
  81.6 12.4 %copy-start.11 = (f32[32,8,128]{2,1,0:T(8,128)S(1)}, f32[32,8,128]{2,1,0:T(8,128)}, u32[]{:S(2)}) copy-start(f32[32,8,128]{2,1,0:T(8,128)} %copy-done.10) | copy-start | bytes 393220
  81.6 12.5 %copy-start.9 = (f32[32,8,128]{2,1,0:T(8,128)S(1)}, f32[32,8,128]{2,1,0:T(8,128)}, u32[]{:S(2)}) copy-start(f32[32,8,128]{2,1,0:T(8,128)} %copy-done.8) | copy-start | bytes 393220
  81.6 312.3 %all-reduce.5.cloned.1.call-start = ((), (), s32[]{:S(2)}) async-start(), calls=%async_computation.1 | async-start | bytes 3145728 | tf_op jit(solution)/shard_map/psum | solution.py:278
  85.6 29.3 %copy-start.12 = (f32[2,128,128]{2,1,0:T(8,128)}, f32[2,128,128]{2,1,0:T(8,128)S(1)}, u32[]{:S(2)}) copy-start(f32[2,128,128]{2,1,0:T(8,128)S(1)} %fusion.18) | copy-start | bytes 393220
  85.6 8.6 %collective-permute-start.9 = (f32[2,64,128]{2,1,0:T(8,128)S(1)}, f32[2,64,128]{2,1,0:T(8,128)S(1)}, u32[]{:S(2)}, u32[]{:S(2)}) collective-permute-start(f32[2,64,128]{2,1,0:T(8,128)S(1)} %get-tuple-element.45), channel_id=1, source_target_pairs={{8,0},{16,8},{24,16},{9,1},{17,9},{25,17},{10,2},{18,10},{26,18},{... | collective-permute-start | bytes 196616 | tf_op jit(solution)/shard_map/ppermute | solution.py:28
  92.7 4.7 %collective-permute-start.8 = (f32[2,64,128]{2,1,0:T(8,128)S(1)}, f32[2,64,128]{2,1,0:T(8,128)S(1)}, u32[]{:S(2)}, u32[]{:S(2)}) collective-permute-start(f32[2,64,128]{2,1,0:T(8,128)S(1)} %get-tuple-element.44), channel_id=1, source_target_pairs={{0,8},{8,16},{16,24},{1,9},{9,17},{17,25},{2,10},{10,18},{18,26},{... | collective-permute-start | bytes 196616 | tf_op jit(solution)/shard_map/ppermute | solution.py:25
  97.6 9.2 %collective-permute-start.11 = (f32[2,256,64]{2,1,0:T(8,128)S(1)}, f32[2,256,64]{2,1,0:T(8,128)S(1)}, u32[]{:S(2)}, u32[]{:S(2)}) collective-permute-start(f32[2,256,64]{2,1,0:T(8,128)S(1)} %get-tuple-element.41), channel_id=1, source_target_pairs={{1,0},{2,1},{3,2},{4,3},{5,4},{6,5},{7,6},{9,8},{10,9},{11,10},{12... | collective-permute-start | bytes 393224 | tf_op jit(solution)/shard_map/ppermute | solution.py:28
  98.9 15.7 %collective-permute-start.10 = (f32[2,256,64]{2,1,0:T(8,128)S(1)}, f32[2,256,64]{2,1,0:T(8,128)S(1)}, u32[]{:S(2)}, u32[]{:S(2)}) collective-permute-start(f32[2,256,64]{2,1,0:T(8,128)S(1)} %get-tuple-element.40), channel_id=1, source_target_pairs={{0,1},{1,2},{2,3},{3,4},{4,5},{5,6},{6,7},{8,9},{9,10},{10,11},{11... | collective-permute-start | bytes 393224 | tf_op jit(solution)/shard_map/ppermute | solution.py:25
  220.6 1.0 copy-start.5
  220.6 1.1 copy-start.7
  242.9 1.1 copy-start.1
  244.2 8.5 %collective-permute-start.13 = (f32[3,64,256]{2,1,0:T(8,128)S(1)}, f32[3,64,256]{2,1,0:T(8,128)S(1)}, u32[]{:S(2)}, u32[]{:S(2)}) collective-permute-start(f32[3,64,256]{2,1,0:T(8,128)S(1)} %slice.172), channel_id=1, source_target_pairs={{8,0},{16,8},{24,16},{9,1},{17,9},{25,17},{10,2},{18,10},{26,18},{... | collective-permute-start | bytes 589832 | tf_op jit(solution)/shard_map/ppermute | solution.py:251
  252.7 11.8 %collective-permute-start.12 = (f32[3,64,256]{2,1,0:T(8,128)S(1)}, f32[3,64,256]{2,1,0:T(8,128)S(1)}, u32[]{:S(2)}, u32[]{:S(2)}) collective-permute-start(f32[3,64,256]{2,1,0:T(8,128)S(1)} %get-tuple-element.29), channel_id=1, source_target_pairs={{0,8},{8,16},{16,24},{1,9},{9,17},{17,25},{2,10},{10,18},{18,26},{... | collective-permute-start | bytes 589832 | tf_op jit(solution)/shard_map/ppermute | solution.py:252
  254.2 23.5 %copy-start.13 = (f32[2,128,128]{2,1,0:T(8,128)S(1)}, f32[2,128,128]{2,1,0:T(8,128)}, u32[]{:S(2)}) copy-start(f32[2,128,128]{2,1,0:T(8,128)} %copy-done.12) | copy-start | bytes 393220
  264.6 7.6 %collective-permute-start.15 = (f32[3,128,64]{2,1,0:T(8,128)S(1)}, f32[3,128,64]{2,1,0:T(8,128)S(1)}, u32[]{:S(2)}, u32[]{:S(2)}) collective-permute-start(f32[3,128,64]{2,1,0:T(8,128)S(1)} %get-tuple-element.34), channel_id=1, source_target_pairs={{1,0},{2,1},{3,2},{4,3},{5,4},{6,5},{7,6},{9,8},{10,9},{11,10},{12... | collective-permute-start | bytes 294920 | tf_op jit(solution)/shard_map/ppermute | solution.py:251
  265.9 11.6 %collective-permute-start.14 = (f32[3,128,64]{2,1,0:T(8,128)S(1)}, f32[3,128,64]{2,1,0:T(8,128)S(1)}, u32[]{:S(2)}, u32[]{:S(2)}) collective-permute-start(f32[3,128,64]{2,1,0:T(8,128)S(1)} %get-tuple-element.35), channel_id=1, source_target_pairs={{0,1},{1,2},{2,3},{3,4},{4,5},{5,6},{6,7},{8,9},{9,10},{10,11},{11... | collective-permute-start | bytes 294920 | tf_op jit(solution)/shard_map/ppermute | solution.py:252
Sparse Core Ops, SparseCore 0:
  81.7 137.2 all-reduce.2
  254.1 139.7 all-reduce.4

commit v2 on v1

--- a/solution.py
+++ b/solution.py
@@ -15,19 +15,6 @@
 
 amp_floor = 0.5
 count_scale = 0.03125
-
-
-def extended_2(block, sides, width):
-    for axis, dim in sides:
-        count = lax.axis_size(axis)
-        forward = [(i, i + 1) for i in range(count - 1)]
-        backward = [(target, source) for source, target in forward]
-        low = lax.ppermute(
-            lax.slice_in_dim(block, block.shape[dim] - width, None, axis=dim), axis, forward
-        )
-        high = lax.ppermute(lax.slice_in_dim(block, 0, width, axis=dim), axis, backward)
-        block = jnp.concatenate([low, block, high], axis=dim)
-    return block
 
 
 def halves(values):
@@ -70,7 +57,7 @@
     count_ref, offs_ref, coef_ref, ext_ref, modes_ref, photon_ref, fr_ref, fl_ref, br_ref, bl_ref,
     acc_ref, mom_ref, num_ref, den_ref, obj_s, prb_s, psi_s, cross_s, power_s,
 ):
-    modes, _, size, _ = modes_ref.shape
+    _, modes, size, _ = modes_ref.shape
     extent = 2 * size
     step = 16
     chunks = size // step
@@ -79,7 +66,7 @@
     num_ref[...] = jnp.zeros_like(num_ref)
     den_ref[...] = jnp.zeros_like(den_ref)
     for k in range(modes):
-        re, im = modes_ref[k, 0], modes_ref[k, 1]
+        re, im = modes_ref[0, k], modes_ref[1, k]
         power_s[k] = re * re + im * im
     lane = lax.broadcasted_iota(jnp.int32, (size, size), 1)
     live = count_ref[0]
@@ -93,7 +80,7 @@
         def probe_rows(chunk, carry):
             rows = pl.ds(pl.multiple_of(chunk * 8, 8), 8)
             for comp in range(2):
-                parts = [modes_ref[k, comp, rows, :] for k in range(modes)]
+                parts = [modes_ref[comp, k, rows, :] for k in range(modes)]
                 for g in range(GROUP):
                     total = weights[g][0] * parts[0]
                     for k in range(1, modes):
@@ -165,7 +152,7 @@
 
             def rows_sums(chunk, sums):
                 rows = pl.ds(pl.multiple_of(chunk * step, step), step)
-                re, im, power = modes_ref[k, 0, rows, :], modes_ref[k, 1, rows, :], power_s[k, rows, :]
+                re, im, power = modes_ref[0, k, rows, :], modes_ref[1, k, rows, :], power_s[k, rows, :]
                 totals = [mom_ref[c, k, rows, :] for c in range(3)]
                 new = []
                 for g in range(GROUP):
@@ -224,62 +211,332 @@
     )(count, offs, coef, ext, modes, photons, *tables)
 
 
-def fold_edges(padded, margin):
-    tile_width = padded.shape[1] - 4 * margin
-    lower_edge = 2 * margin
-    upper_edge = tile_width + 2 * margin
-    outer_edge = tile_width + 3 * margin
-    inner_end = tile_width - margin
-    interior = padded[:, lower_edge:upper_edge, lower_edge:upper_edge]
-    interior = interior.at[:, :margin, :].add(padded[:, :margin, lower_edge:upper_edge])
-    interior = interior.at[:, inner_end:, :].add(padded[:, outer_edge:, lower_edge:upper_edge])
-    interior = interior.at[:, :, :margin].add(padded[:, lower_edge:upper_edge, :margin])
-    interior = interior.at[:, :, inner_end:].add(padded[:, lower_edge:upper_edge, outer_edge:])
-    interior = interior.at[:, :margin, :margin].add(padded[:, :margin, :margin])
-    interior = interior.at[:, :margin, inner_end:].add(padded[:, :margin, outer_edge:])
-    interior = interior.at[:, inner_end:, :margin].add(padded[:, outer_edge:, :margin])
-    interior = interior.at[:, inner_end:, inner_end:].add(padded[:, outer_edge:, outer_edge:])
-    return interior
-
-
-def folded(block, sides, width):
-    for axis, dim in sides:
-        count = lax.axis_size(axis)
-        forward = [(i, i + 1) for i in range(count - 1)]
-        backward = [(target, source) for source, target in forward]
-        size = block.shape[dim] - 2 * width
-        low = lax.ppermute(lax.slice_in_dim(block, 0, width, axis=dim), axis, backward)
-        high = lax.ppermute(lax.slice_in_dim(block, size + width, None, axis=dim), axis, forward)
-        inner = lax.slice_in_dim(block, width, size + width, axis=dim)
-        first = lax.slice_in_dim(inner, 0, width, axis=dim) + high
-        last = lax.slice_in_dim(inner, size - width, None, axis=dim) + low
-        middle = lax.slice_in_dim(inner, width, size - width, axis=dim)
-        block = jnp.concatenate([first, middle, last], axis=dim)
-    return block
+def edge_copies(src_low, dst_low, src_high, dst_high, axis, sems):
+    place = {name: lax.axis_index(name) for name in ("row", "col")}
+    here, count = place[axis], lax.axis_size(axis)
+    send_sem, recv_sem, first = sems
+    copies = []
+    for number, (src, dst, to) in enumerate(
+        ((src_low, dst_low, jnp.maximum(here - 1, 0)), (src_high, dst_high, jnp.minimum(here + 1, count - 1)))
+    ):
+        target = dict(place)
+        target[axis] = to
+        copies.append(
+            pltpu.make_async_remote_copy(
+                src_ref=src,
+                dst_ref=dst,
+                send_sem=send_sem.at[first + number],
+                recv_sem=recv_sem.at[first + number],
+                device_id=(target["row"], target["col"]),
+                device_id_type=pl.DeviceIdType.MESH,
+            )
+        )
+    below, above = here > 0, here < count - 1
+
+    def start():
+        pl.when(below)(copies[0].start)
+        pl.when(above)(copies[1].start)
+
+    def arrive():
+        pl.when(above)(copies[0].wait_recv)
+        pl.when(below)(copies[1].wait_recv)
+
+    def finish():
+        pl.when(below)(copies[0].wait_send)
+        pl.when(above)(copies[1].wait_send)
+
+    return start, arrive, finish
+
+
+def exchange_kernel(has_fold, has_halo, *refs):
+    refs = list(refs)
+    obj_ref = refs.pop(0)
+    if has_fold:
+        acc_ref, mom_ref, modes_ref = refs[:3]
+        obj_out, modes_out = refs[3:5]
+        refs = refs[5:]
+    if has_halo:
+        ext_ref = refs.pop(0)
+    send_sem, recv_sem = refs[:2]
+    refs = refs[2:]
+    if has_halo:
+        q_s, qlow_s, qhigh_s = refs[:3]
+        refs = refs[3:]
+    if has_fold:
+        up_s, down_s, mid_s, fromlow_s, fromhigh_s, buf1, sum1, buf2, sum2, buf3 = refs
+
+    row, col = lax.axis_index("row"), lax.axis_index("col")
+    rows_n, cols_n = lax.axis_size("row"), lax.axis_size("col")
+    size = obj_ref.shape[-1]
+    margin = size // 2
+    tile_end = margin + size
+
+    barrier = pltpu.get_barrier_semaphore()
+    for step in range(1, rows_n):
+        pl.semaphore_signal(
+            barrier, inc=1, device_id=(lax.rem(row + step, rows_n), col), device_id_type=pl.DeviceIdType.MESH
+        )
+    for step in range(1, cols_n):
+        pl.semaphore_signal(
+            barrier, inc=1, device_id=(row, lax.rem(col + step, cols_n)), device_id_type=pl.DeviceIdType.MESH
+        )
+    pl.semaphore_wait(barrier, rows_n + cols_n - 2)
+
+    used = [0]
+
+    def take(count):
+        first = used[0]
+        used[0] += count
+        return first
+
+    def copy(src, dst, device, number):
+        return pltpu.make_async_remote_copy(
+            src_ref=src,
+            dst_ref=dst,
+            send_sem=send_sem.at[number],
+            recv_sem=recv_sem.at[number],
+            device_id=device,
+            device_id_type=pl.DeviceIdType.MESH,
+        )
+
+    finishing = []
+    lane = lax.broadcasted_iota(jnp.int32, (size, size), 1)
+    upper = lane >= margin
+
+    if has_fold:
+        total_rows = mom_ref.shape[1]
+        core, line, lines = lax.rem(row, 2), row // 2, rows_n // 2
+        half_rows = total_rows // 2
+        line_rows = half_rows // lines
+        own_rows = line_rows // cols_n
+        half_at = pl.multiple_of(core * half_rows, half_rows)
+        other_at = pl.multiple_of((1 - core) * half_rows, half_rows)
+        line_at = pl.multiple_of(half_at + line * line_rows, line_rows)
+        own_at = pl.multiple_of(line_at + col * own_rows, own_rows)
+        partner = (line * 2 + 1 - core, col)
+
+        pair = copy(mom_ref.at[:, pl.ds(other_at, half_rows), :], buf1, partner, take(1))
+        pair.start()
+        start, arrive, finish = edge_copies(
+            acc_ref.at[:, pl.ds(0, margin), :], down_s,
+            acc_ref.at[:, pl.ds(tile_end, margin), :], up_s,
+            "row", (send_sem, recv_sem, take(2)),
+        )
+
+        @pl.when(row == 0)
+        def _():
+            up_s[...] = jnp.zeros_like(up_s)
+
+        @pl.when(row == rows_n - 1)
+        def _():
+            down_s[...] = jnp.zeros_like(down_s)
+
+        @pl.when(col == 0)
+        def _():
+            fromlow_s[...] = jnp.zeros_like(fromlow_s)
+
+        @pl.when(col == cols_n - 1)
+        def _():
+            fromhigh_s[...] = jnp.zeros_like(fromhigh_s)
+
+        start()
+        finishing += [finish, pair.wait_send]
+
+        pair.wait_recv()
+        sum1[...] = mom_ref[:, pl.ds(half_at, half_rows), :] + buf1[...]
+        first = take(lines - 1)
+        line_copies = []
+        for step in range(1, lines):
+            to = lax.rem(line + step, lines)
+            at = pl.multiple_of(to * line_rows, line_rows)
+            line_copies.append(
+                copy(sum1.at[:, pl.ds(at, line_rows), :], buf2.at[step - 1], (to * 2 + core, col), first + step - 1)
+            )
+            line_copies[-1].start()
+
+        arrive()
+        for comp in range(3):
+            for half in range(2):
+                plane = 2 * comp + half
+                mid_s[half, comp, :margin, :] = acc_ref[plane, margin:size, :] + up_s[plane]
+                mid_s[half, comp, margin:, :] = acc_ref[plane, size:tile_end, :] + down_s[plane]
+        start, arrive, finish = edge_copies(
+            mid_s.at[0], fromhigh_s, mid_s.at[1], fromlow_s, "col", (send_sem, recv_sem, take(2))
+        )
+        start()
+        finishing.append(finish)
+
+        total = sum1[:, pl.ds(pl.multiple_of(line * line_rows, line_rows), line_rows), :]
+        for step in range(1, lines):
+            line_copies[step - 1].wait_recv()
+            total = total + buf2[step - 1]
+        sum2[...] = total
+        first = take(cols_n - 1)
+        col_copies = []
+        for step in range(1, cols_n):
+            to = lax.rem(col + step, cols_n)
+            at = pl.multiple_of(to * own_rows, own_rows)
+            col_copies.append(copy(sum2.at[:, pl.ds(at, own_rows), :], buf3.at[step - 1], (row, to), first + step - 1))
+            col_copies[-1].start()
+        finishing += [c.wait_send for c in line_copies + col_copies]
+
+        arrive()
+        parts = [
+            jnp.where(upper, mid_s[0, c] + fromlow_s[c], mid_s[1, c] + fromhigh_s[c]) for c in range(3)
+        ]
+        for c in range(2):
+            new = pltpu.roll(obj_ref[c], margin, 1) + parts[c] / (parts[2] + 1.0)
+            if has_halo:
+                q_s[c] = new
+            obj_out[c] = pltpu.roll(new, margin, 1)
+    else:
+        for c in range(2):
+            q_s[c] = pltpu.roll(obj_ref[c], margin, 1)
+
+    if has_halo:
+
+        @pl.when(col == 0)
+        def _():
+            qlow_s[...] = jnp.zeros_like(qlow_s)
+
+        @pl.when(col == cols_n - 1)
+        def _():
+            qhigh_s[...] = jnp.zeros_like(qhigh_s)
+
+        start, arrive, finish = edge_copies(q_s, qhigh_s, q_s, qlow_s, "col", (send_sem, recv_sem, take(2)))
+        start()
+        finishing.append(finish)
+
+    if has_fold:
+        total = sum2[:, pl.ds(pl.multiple_of(col * own_rows, own_rows), own_rows), :]
+        for step in range(1, cols_n):
+            col_copies[step - 1].wait_recv()
+            total = total + buf3[step - 1]
+        own = pl.ds(own_at, own_rows)
+        for c in range(2):
+            modes_out[c, own, :] = modes_ref[c, own, :] + total[c] / (total[2] + 1.0)
+        first = take(cols_n - 1)
+        back_cols = []
+        for step in range(1, cols_n):
+            part = modes_out.at[:, own, :]
+            back_cols.append(copy(part, part, (row, lax.rem(col + step, cols_n)), first + step - 1))
+            back_cols[-1].start()
+        finishing += [c.wait_send for c in back_cols]
+
+    if has_halo:
+        arrive()
+        for c in range(2):
+            ext_ref[2 * c, margin:tile_end, :] = jnp.where(upper, q_s[c], qlow_s[c])
+            ext_ref[2 * c + 1, margin:tile_end, :] = jnp.where(upper, qhigh_s[c], q_s[c])
+
+        @pl.when(row == 0)
+        def _():
+            ext_ref[:, :margin, :] = jnp.zeros((4, margin, size), jnp.float32)
+
+        @pl.when(row == rows_n - 1)
+        def _():
+            ext_ref[:, tile_end:, :] = jnp.zeros((4, margin, size), jnp.float32)
+
+        start, arrive, finish = edge_copies(
+            ext_ref.at[:, pl.ds(margin, margin), :], ext_ref.at[:, pl.ds(tile_end, margin), :],
+            ext_ref.at[:, pl.ds(size, margin), :], ext_ref.at[:, pl.ds(0, margin), :],
+            "row", (send_sem, recv_sem, take(2)),
+        )
+        start()
+        finishing.append(finish)
+
+    if has_fold:
+        for c in back_cols:
+            c.wait_recv()
+        first = take(lines - 1)
+        back_lines = []
+        for step in range(1, lines):
+            part = modes_out.at[:, pl.ds(line_at, line_rows), :]
+            to = lax.rem(line + step, lines)
+            back_lines.append(copy(part, part, (to * 2 + core, col), first + step - 1))
+            back_lines[-1].start()
+        for c in back_lines:
+            c.wait_recv()
+        part = modes_out.at[:, pl.ds(half_at, half_rows), :]
+        pair = copy(part, part, partner, take(1))
+        pair.start()
+        pair.wait_recv()
+        finishing += [c.wait_send for c in back_lines + [pair]]
+    if has_halo:
+        arrive()
+    for finish in finishing:
+        finish()
+
+
+def exchange_call(has_fold, has_halo, number, obj, acc=None, moments=None, modes=None):
+    f32 = jnp.float32
+    size = obj.shape[-1]
+    margin = size // 2
+    rows_n, cols_n = lax.axis_size("row"), lax.axis_size("col")
+    vmem = pl.BlockSpec(memory_space=pltpu.VMEM)
+    outs, scratch, inputs = [], [], [obj]
+    sems = 0
+    if has_fold:
+        inputs += [acc, moments, modes]
+        outs += [jax.ShapeDtypeStruct(obj.shape, f32), jax.ShapeDtypeStruct(modes.shape, f32)]
+        sems += 6 + 2 * (rows_n // 2 - 1) + 2 * (cols_n - 1)
+    if has_halo:
+        outs.append(jax.ShapeDtypeStruct((4, 2 * size, size), f32))
+        sems += 4
+    scratch += [pltpu.SemaphoreType.DMA((sems,))] * 2
+    if has_halo:
+        scratch += [pltpu.VMEM((2, size, size), f32)] * 3
+    if has_fold:
+        half_rows = moments.shape[1] // 2
+        lines = rows_n // 2
+        line_rows = half_rows // lines
+        own_rows = line_rows // cols_n
+        scratch += [
+            pltpu.VMEM((6, margin, size), f32),
+            pltpu.VMEM((6, margin, size), f32),
+            pltpu.VMEM((2, 3, size, size), f32),
+            pltpu.VMEM((3, size, size), f32),
+            pltpu.VMEM((3, size, size), f32),
+            pltpu.VMEM((3, half_rows, size), f32),
+            pltpu.VMEM((3, half_rows, size), f32),
+            pltpu.VMEM((max(lines - 1, 1), 3, line_rows, size), f32),
+            pltpu.VMEM((3, line_rows, size), f32),
+            pltpu.VMEM((cols_n - 1, 3, own_rows, size), f32),
+        ]
+    return pl.pallas_call(
+        functools.partial(exchange_kernel, has_fold, has_halo),
+        out_shape=tuple(outs),
+        in_specs=[vmem] * len(inputs),
+        out_specs=(vmem,) * len(outs),
+        scratch_shapes=scratch,
+        compiler_params=pltpu.CompilerParams(
+            collective_id=number, has_side_effects=True, vmem_limit_bytes=VMEM_LIMIT
+        ),
+        name=f"exchange{number}",
+    )(*inputs)
 
 
 def shards(object_field, probe_modes, coefficients, offsets, counts, measured):
     size = measured.shape[-1]
-    margin = size // 2
-    extent = object_field.shape[1] + size
+    kinds = probe_modes.shape[0]
     tables = dft_tables(size)
     coef = coefficients[0, 0]
-    sides = (("row", 1), ("col", 2))
+    modes = probe_modes.transpose(1, 0, 2, 3)
+    (ext,) = exchange_call(False, True, 0, object_field)
     for iteration in range(ITERS):
-        extended = extended_2(object_field, sides, margin)
-        ext = extended.reshape(2, extent, 2, size).transpose(0, 2, 1, 3).reshape(-1, size)
         acc, moments, num, den = positions_call(
-            counts[0], offsets[0, 0], coef, ext, probe_modes, measured[0, 0], tables
+            counts[0], offsets[0, 0], coef, ext.reshape(-1, size), modes, measured[0, 0], tables
         )
         coef = coef + num.sum(axis=-1) / (den.sum(axis=-1) + 1.0)
-        acc = acc.reshape(3, 2, extent, size).transpose(0, 2, 1, 3).reshape(3, extent, extent)
-        interior = folded(acc, sides, margin)
-        object_field = object_field + interior[0:2] / (interior[2:3] + 1.0)
-        totals = lax.psum(moments, ("row", "col"))
-        probe_modes = probe_modes + jnp.stack([totals[0], totals[1]], axis=1) / (
-            totals[2][:, None] + 1.0
-        )
-    return (object_field, probe_modes, coef[None, None])
+        more = iteration < ITERS - 1
+        results = exchange_call(
+            True, more, 1 if more else 2, object_field,
+            acc.reshape(6, -1, size), moments.reshape(3, -1, size), modes.reshape(2, -1, size),
+        )
+        object_field, modes = results[0], results[1].reshape(2, kinds, size, size)
+        if more:
+            ext = results[2]
+    return (object_field, modes.transpose(1, 0, 2, 3), coef[None, None])
 
 
 def solution(mesh):

time: 408 us -> 177 us (0.43); the launches traced: 403 us -> 177 us
  waiting for transfers between devices: 280 us -> 0 us
  Pallas kernels: 43.6 us -> 162 us
  starting transfers between devices: 51.9 us -> 0 us
  between operations: 15.3 us -> 1.53 us
  local copies, waits for them, and re-layouts: 6.04 us -> 12.7 us
  other arithmetic: 7.01 us -> 0.44 us
    psum x2 -> x0, waiting for transfers between devices: 220 us -> none  [shards(): totals = lax.psum(moments, ('row', 'col'))]
    pallas_call x0 -> x3, Pallas kernels: none -> 120 us  [exchange_call(): pl.pallas_call(functools.partial(exchange_kernel, has_fold, has_halo), ou...]
    ppermute x16 -> x0, waiting for transfers between devices: 60 us -> none  [the longest x4 31.6 us: folded(): lax.ppermute(lax.slice_in_dim(block, size + width, None, axis=dim), axis,...]
    ppermute x16 -> x0, starting transfers between devices: 51.8 us -> none  [the longest x4 16.6 us: folded(): lax.ppermute(lax.slice_in_dim(block, 0, width, axis=dim), axis, backward)]
    unnamed x38 -> x34, local copies, waits for them, and re-layouts: 3.76 us -> 11.5 us
    add x12 -> x0, other arithmetic: 5.63 us -> none  [the longest x2 2.99 us: shards(): totals[2][:, None] + 1.0]
  transfers between devices with their start and end apart: 18 -> 0, of which waited for: 15 -> 0; matrix products, arithmetic and copies ran while one was open for 1% -> 0% of each run, Pallas kernels for 0% -> 0%
where the time goes in v2:
time: 177 us
  Pallas kernels  162 us (92%)
  local copies, waits for them, and re-layouts  12.7 us (7%)
    pallas_call x3, Pallas kernels, exchange_call(): pl.pallas_call(functools.partial(exchange_kernel, has_fold, has_halo), ou...  120 us
    pallas_call x2, Pallas kernels, positions_call(): pl.pallas_call(positions_kernel, out_shape=(jax.ShapeDtypeStruct((6 * ext...  42.4 us
    unnamed x34, local copies, waits for them, and re-layouts  11.5 us

profile of v2, /device:TPU:5, one launch (start us, length us, event | category | flops | bytes accessed | tf_op | source)
XLA Modules:
  0.0 177.0 jit_solution(14766372617269752846)
XLA Ops:
  0.6 0.0 copy-start.4
  0.6 0.0 copy-start.5
  0.7 0.0 copy-start.6
  0.7 0.0 copy-start.7
  0.7 0.0 copy-start.14
  0.7 0.0 copy-start.11
  0.7 0.9 copy.13
  1.6 1.3 copy.24
  2.9 0.0 copy-done.14
  2.9 0.1 copy.15.offs_ref
  3.6 0.0 copy-done.11
  3.6 10.5 %exchange0.1 = f32[4,256,128]{2,1,0:T(8,128)S(1)} custom-call(f32[2,128,128]{2,1,0:T(8,128)S(1)} %copy-done.11), custom_call_target="tpu_custom_call" | custom-call | tf_op jit(solution)/shard_map/exchange0/pallas_call | solution.py:506
  14.2 0.0 copy-done.4
  14.2 0.0 copy-done.5
  14.2 0.0 copy-done.6
  14.2 0.0 copy-done.7
  14.2 21.2 %positions.2 = (f32[1536,128]{1,0:T(8,128)S(1)}, f32[3,8,128,128]{3,2,1,0:T(8,128)S(1)}, f32[32,8,128]{2,1,0:T(8,128)S(1)}, f32[32,8,128]{2,1,0:T(8,128)S(1)}) custom-call(s32[1]{0:T(128)} %bitcast.26.count_ref, s32[32,2]{1,0:T(8,128)S(1)} %copy.15.offs_ref, f32[32,8]{1,0:T(8,128)S(1)} %bitcast.38, f32[1024,128]{1,0:T(8,128)S(1)} %bitcast.31, ...), custom_call_target="tpu_custom_call" | custom-call | tf_op jit(solution)/shard_map/positions/pallas_call | solution.py:192
  35.4 0.0 copy-start.2
  35.4 1.1 copy-done.2
  36.5 0.0 copy-start.9
  36.5 0.9 copy-done.9
  37.4 0.1 reduce_sum.36
  37.5 0.1 reduce_sum.37
  37.7 0.0 copy-start.3
  37.7 1.4 copy-done.3
  39.1 0.0 copy-start.10
  39.1 1.1 copy-done.10
  40.2 0.0 copy-start.8
  40.2 54.9 %exchange1.1 = (f32[2,128,128]{2,1,0:T(8,128)S(1)}, f32[2,1024,128]{2,1,0:T(8,128)S(1)}, f32[4,256,128]{2,1,0:T(8,128)S(1)}) custom-call(f32[2,128,128]{2,1,0:T(8,128)S(1)} %copy-done.11, f32[6,256,128]{2,1,0:T(8,128)S(1)} %bitcast.36, f32[3,1024,128]{2,1,0:T(8,128)S(1)} %bitcast.33, f32[2,1024,128]{2,1,0:T(8,128)S(1)} %bitcast.29), custom_call_target="tpu_custom_call" | custom-call | tf_op jit(solution)/shard_map/exchange1/pallas_call | solution.py:506
  95.1 0.0 copy-start.12
  95.2 0.0 copy-done.8
  95.2 21.2 %positions.3 = (f32[1536,128]{1,0:T(8,128)S(1)}, f32[3,8,128,128]{3,2,1,0:T(8,128)S(1)}, f32[32,8,128]{2,1,0:T(8,128)S(1)}, f32[32,8,128]{2,1,0:T(8,128)S(1)}) custom-call(s32[1]{0:T(128)} %bitcast.27.count_ref, s32[32,2]{1,0:T(8,128)S(1)} %copy.15.offs_ref, f32[32,8]{1,0:T(8,128)S(1)} %bitcast_add_fusion.2.coef_ref, f32[1024,128]{1,0:T(8,128)S(1)} %bitcast.37, ...), custom_call_target="tpu_custom_call" | custom-call | tf_op jit(solution)/shard_map/positions/pallas_call | solution.py:192
  116.4 0.0 copy-done.12
  116.4 0.0 copy-start
  116.4 1.1 copy-done
  117.5 0.1 reduce_sum.38
  117.7 0.1 reduce_sum.39
  117.8 0.7 copy.19
  118.5 0.0 copy-start.1
  118.5 1.4 copy-done.1
  119.9 0.0 copy-start.13
  119.9 0.9 copy-done.13
  120.8 54.5 %exchange2.1 = (f32[2,128,128]{2,1,0:T(8,128)S(1)}, f32[2,1024,128]{2,1,0:T(8,128)S(1)}) custom-call(f32[2,128,128]{2,1,0:T(8,128)S(1)} %copy-done.13, f32[6,256,128]{2,1,0:T(8,128)S(1)} %bitcast.35, f32[3,1024,128]{2,1,0:T(8,128)S(1)} %bitcast.32, f32[2,1024,128]{2,1,0:T(8,128)S(1)} %get-tuple-element.22.refs_3_), custom_call_target="tpu_custom_call" | custom-call | tf_op jit(solution)/shard_map/exchange2/pallas_call | solution.py:506
  175.3 1.1 copy.23
  176.3 0.7 copy.27
  (2 shorter events, 0.0 us)
Async XLA Ops:
  0.6 13.5 %copy-start.4 = (bf16[768,256]{1,0:T(8,128)(2,1)S(1)}, bf16[768,256]{1,0:T(8,128)(2,1)}, u32[]{:S(2)}) copy-start(bf16[768,256]{1,0:T(8,128)(2,1)} %constant.18.fr_ref) | copy-start | bytes 1179652
  0.6 13.5 %copy-start.5 = (bf16[256,768]{1,0:T(8,128)(2,1)S(1)}, bf16[256,768]{1,0:T(8,128)(2,1)}, u32[]{:S(2)}) copy-start(bf16[256,768]{1,0:T(8,128)(2,1)} %constant.23.fl_ref) | copy-start | bytes 1179652
  0.7 13.5 %copy-start.6 = (bf16[768,256]{1,0:T(8,128)(2,1)S(1)}, bf16[768,256]{1,0:T(8,128)(2,1)}, u32[]{:S(2)}) copy-start(bf16[768,256]{1,0:T(8,128)(2,1)} %constant.24.br_ref) | copy-start | bytes 1179652
  0.7 13.5 %copy-start.7 = (bf16[256,768]{1,0:T(8,128)(2,1)S(1)}, bf16[256,768]{1,0:T(8,128)(2,1)}, u32[]{:S(2)}) copy-start(bf16[256,768]{1,0:T(8,128)(2,1)} %constant.25.bl_ref) | copy-start | bytes 1179652
  0.7 2.2 %copy-start.14 = (s32[1,1,32,2]{2,3,1,0:T(2,128)S(1)}, s32[1,1,32,2]{2,3,1,0:T(2,128)}, u32[]{:S(2)}) copy-start(s32[1,1,32,2]{2,3,1,0:T(2,128)} %param.13) | copy-start | bytes 772
  0.7 2.9 %copy-start.11 = (f32[2,128,128]{2,1,0:T(8,128)S(1)}, f32[2,128,128]{2,1,0:T(8,128)}, u32[]{:S(2)}) copy-start(f32[2,128,128]{2,1,0:T(8,128)} %refs_0_.3) | copy-start | bytes 393220
  35.4 1.1 copy-start.2
  36.5 0.9 copy-start.9
  37.7 1.4 copy-start.3
  39.1 1.1 copy-start.10
  40.2 55.0 %copy-start.8 = (bf16[256,768]{1,0:T(8,128)(2,1)S(1)}, bf16[256,768]{1,0:T(8,128)(2,1)}, u32[]{:S(2)}) copy-start(bf16[256,768]{1,0:T(8,128)(2,1)} %constant.25.bl_ref) | copy-start | bytes 1179652
  95.1 21.3 %copy-start.12 = (f32[2,128,128]{2,1,0:T(8,128)}, f32[2,128,128]{2,1,0:T(8,128)S(1)}, u32[]{:S(2)}) copy-start(f32[2,128,128]{2,1,0:T(8,128)S(1)} %get-tuple-element.18.refs_0_) | copy-start | bytes 393220
  116.4 1.1 copy-start
  118.5 1.4 copy-start.1
  119.9 0.9 copy-start.13

commit v3 on v2

--- a/solution.py
+++ b/solution.py
@@ -11,7 +11,7 @@
 
 ITERS = 2
 GROUP = 4
-VMEM_LIMIT = 48 * 1024 * 1024
+VMEM_LIMIT = 20 * 1024 * 1024
 
 amp_floor = 0.5
 count_scale = 0.03125
@@ -315,8 +315,13 @@
         own_at = pl.multiple_of(line_at + col * own_rows, own_rows)
         partner = (line * 2 + 1 - core, col)
 
-        pair = copy(mom_ref.at[:, pl.ds(other_at, half_rows), :], buf1, partner, take(1))
-        pair.start()
+        planes = (2, 0, 1)
+        first = take(3)
+        pairs = [
+            copy(mom_ref.at[p, pl.ds(other_at, half_rows), :], buf1.at[p], partner, first + p) for p in range(3)
+        ]
+        for p in planes:
+            pairs[p].start()
         start, arrive, finish = edge_copies(
             acc_ref.at[:, pl.ds(0, margin), :], down_s,
             acc_ref.at[:, pl.ds(tile_end, margin), :], up_s,
@@ -340,19 +345,20 @@
             fromhigh_s[...] = jnp.zeros_like(fromhigh_s)
 
         start()
-        finishing += [finish, pair.wait_send]
-
-        pair.wait_recv()
-        sum1[...] = mom_ref[:, pl.ds(half_at, half_rows), :] + buf1[...]
-        first = take(lines - 1)
-        line_copies = []
-        for step in range(1, lines):
-            to = lax.rem(line + step, lines)
-            at = pl.multiple_of(to * line_rows, line_rows)
-            line_copies.append(
-                copy(sum1.at[:, pl.ds(at, line_rows), :], buf2.at[step - 1], (to * 2 + core, col), first + step - 1)
-            )
-            line_copies[-1].start()
+        finishing += [finish] + [c.wait_send for c in pairs]
+
+        line_copies = {}
+        for p in planes:
+            pairs[p].wait_recv()
+            sum1[p] = mom_ref[p, pl.ds(half_at, half_rows), :] + buf1[p]
+            first = take(lines - 1)
+            for step in range(1, lines):
+                to = lax.rem(line + step, lines)
+                at = pl.multiple_of(to * line_rows, line_rows)
+                line_copies[p, step] = copy(
+                    sum1.at[p, pl.ds(at, line_rows), :], buf2.at[step - 1, p], (to * 2 + core, col), first + step - 1
+                )
+                line_copies[p, step].start()
 
         arrive()
         for comp in range(3):
@@ -366,19 +372,22 @@
         start()
         finishing.append(finish)
 
-        total = sum1[:, pl.ds(pl.multiple_of(line * line_rows, line_rows), line_rows), :]
-        for step in range(1, lines):
-            line_copies[step - 1].wait_recv()
-            total = total + buf2[step - 1]
-        sum2[...] = total
-        first = take(cols_n - 1)
-        col_copies = []
-        for step in range(1, cols_n):
-            to = lax.rem(col + step, cols_n)
-            at = pl.multiple_of(to * own_rows, own_rows)
-            col_copies.append(copy(sum2.at[:, pl.ds(at, own_rows), :], buf3.at[step - 1], (row, to), first + step - 1))
-            col_copies[-1].start()
-        finishing += [c.wait_send for c in line_copies + col_copies]
+        col_copies = {}
+        for p in planes:
+            total = sum1[p, pl.ds(pl.multiple_of(line * line_rows, line_rows), line_rows), :]
+            for step in range(1, lines):
+                line_copies[p, step].wait_recv()
+                total = total + buf2[step - 1, p]
+            sum2[p] = total
+            first = take(cols_n - 1)
+            for step in range(1, cols_n):
+                to = lax.rem(col + step, cols_n)
+                at = pl.multiple_of(to * own_rows, own_rows)
+                col_copies[p, step] = copy(
+                    sum2.at[p, pl.ds(at, own_rows), :], buf3.at[step - 1, p], (row, to), first + step - 1
+                )
+                col_copies[p, step].start()
+        finishing += [c.wait_send for c in (*line_copies.values(), *col_copies.values())]
 
         arrive()
         parts = [
@@ -408,20 +417,23 @@
         finishing.append(finish)
 
     if has_fold:
-        total = sum2[:, pl.ds(pl.multiple_of(col * own_rows, own_rows), own_rows), :]
-        for step in range(1, cols_n):
-            col_copies[step - 1].wait_recv()
-            total = total + buf3[step - 1]
         own = pl.ds(own_at, own_rows)
-        for c in range(2):
-            modes_out[c, own, :] = modes_ref[c, own, :] + total[c] / (total[2] + 1.0)
-        first = take(cols_n - 1)
-        back_cols = []
-        for step in range(1, cols_n):
-            part = modes_out.at[:, own, :]
-            back_cols.append(copy(part, part, (row, lax.rem(col + step, cols_n)), first + step - 1))
-            back_cols[-1].start()
-        finishing += [c.wait_send for c in back_cols]
+        back_cols = {}
+        for p in planes:
+            total = sum2[p, pl.ds(pl.multiple_of(col * own_rows, own_rows), own_rows), :]
+            for step in range(1, cols_n):
+                col_copies[p, step].wait_recv()
+                total = total + buf3[step - 1, p]
+            if p == 2:
+                below = total + 1.0
+                continue
+            modes_out[p, own, :] = modes_ref[p, own, :] + total / below
+            first = take(cols_n - 1)
+            for step in range(1, cols_n):
+                part = modes_out.at[p, own, :]
+                back_cols[p, step] = copy(part, part, (row, lax.rem(col + step, cols_n)), first + step - 1)
+                back_cols[p, step].start()
+        finishing += [c.wait_send for c in back_cols.values()]
 
     if has_halo:
         arrive()
@@ -446,22 +458,25 @@
         finishing.append(finish)
 
     if has_fold:
-        for c in back_cols:
-            c.wait_recv()
-        first = take(lines - 1)
-        back_lines = []
-        for step in range(1, lines):
-            part = modes_out.at[:, pl.ds(line_at, line_rows), :]
-            to = lax.rem(line + step, lines)
-            back_lines.append(copy(part, part, (to * 2 + core, col), first + step - 1))
-            back_lines[-1].start()
-        for c in back_lines:
-            c.wait_recv()
-        part = modes_out.at[:, pl.ds(half_at, half_rows), :]
-        pair = copy(part, part, partner, take(1))
-        pair.start()
-        pair.wait_recv()
-        finishing += [c.wait_send for c in back_lines + [pair]]
+        back_lines, back_pairs = {}, []
+        for c in range(2):
+            for step in range(1, cols_n):
+                back_cols[c, step].wait_recv()
+            first = take(lines - 1)
+            for step in range(1, lines):
+                part = modes_out.at[c, pl.ds(line_at, line_rows), :]
+                to = lax.rem(line + step, lines)
+                back_lines[c, step] = copy(part, part, (to * 2 + core, col), first + step - 1)
+                back_lines[c, step].start()
+        for c in range(2):
+            for step in range(1, lines):
+                back_lines[c, step].wait_recv()
+            part = modes_out.at[c, pl.ds(half_at, half_rows), :]
+            back_pairs.append(copy(part, part, partner, take(1)))
+            back_pairs[-1].start()
+        for pair in back_pairs:
+            pair.wait_recv()
+        finishing += [c.wait_send for c in (*back_lines.values(), *back_pairs)]
     if has_halo:
         arrive()
     for finish in finishing:
@@ -479,7 +494,7 @@
     if has_fold:
         inputs += [acc, moments, modes]
         outs += [jax.ShapeDtypeStruct(obj.shape, f32), jax.ShapeDtypeStruct(modes.shape, f32)]
-        sems += 6 + 2 * (rows_n // 2 - 1) + 2 * (cols_n - 1)
+        sems += 4 + 5 * (1 + rows_n // 2 - 1 + cols_n - 1)
     if has_halo:
         outs.append(jax.ShapeDtypeStruct((4, 2 * size, size), f32))
         sems += 4

time: 177 us -> 179 us (1.011); the launches traced: 177 us -> 177 us
  Pallas kernels: 162 us -> 148 us
  local copies, waits for them, and re-layouts: 12.7 us -> 22.1 us
  other arithmetic: 0.44 us -> 4.92 us
    pallas_call x3, Pallas kernels: 120 us -> 107 us  [exchange_call(): pl.pallas_call(functools.partial(exchange_kernel, has_fold, has_halo), ou...]
    unnamed x34 -> x52, local copies, waits for them, and re-layouts: 11.5 us -> 19.7 us
    reduce_sum x4, other arithmetic: 0.41 us -> 3.42 us  [shards(): coef = coef + num.sum(axis=-1) / (den.sum(axis=-1) + 1.0)]
where the time goes in v3:
time: 179 us; the launch traced here: 177 us
  Pallas kernels  148 us (83%)
  local copies, waits for them, and re-layouts  22.1 us (12%)
  other arithmetic  4.92 us (3%)
    pallas_call x3, Pallas kernels, exchange_call(): pl.pallas_call(functools.partial(exchange_kernel, has_fold, has_halo), ou...  107 us
    pallas_call x2, Pallas kernels, positions_call(): pl.pallas_call(positions_kernel, out_shape=(jax.ShapeDtypeStruct((6 * ext...  41.3 us
    unnamed x52, local copies, waits for them, and re-layouts  19.7 us

profile of v3, /device:TPU:5, one launch (start us, length us, event | category | flops | bytes accessed | tf_op | source)
XLA Modules:
  0.0 176.7 jit_solution(9450697511327687984)
XLA Ops:
  0.6 0.0 copy-start.7
  0.6 0.0 copy-start
  0.7 0.9 copy.13
  1.6 1.3 copy.24
  2.9 1.4 copy.15.offs_ref
  4.9 0.0 copy-start.16
  4.9 0.9 copy-done.16
  5.8 10.5 %exchange0.1 = f32[4,256,128]{2,1,0:T(8,128)S(1)} custom-call(f32[2,128,128]{2,1,0:T(8,128)S(1)} %copy-done.16), custom_call_target="tpu_custom_call" | custom-call | tf_op jit(solution)/shard_map/exchange0/pallas_call | solution.py:521
  16.3 0.0 copy-done.7
  16.3 0.0 copy-done
  16.3 0.0 copy-start.8
  16.3 1.0 copy-done.8
  17.3 1.0 copy-done.10
  18.3 1.0 copy-done.12
  19.3 0.7 copy-done.18
  20.0 20.6 %positions.2 = (f32[1536,128]{1,0:T(8,128)S(1)}, f32[3,8,128,128]{3,2,1,0:T(8,128)S(1)}, f32[32,8,128]{2,1,0:T(8,128)S(1)}, f32[32,8,128]{2,1,0:T(8,128)S(1)}) custom-call(s32[1]{0:T(128)} %bitcast.26.count_ref, s32[32,2]{1,0:T(8,128)S(1)} %copy-done.18, f32[32,8]{1,0:T(8,128)S(1)} %bitcast.40, f32[1024,128]{1,0:T(8,128)S(1)} %bitcast.33, ...), custom_call_target="tpu_custom_call" | custom-call | tf_op jit(solution)/shard_map/positions/pallas_call | solution.py:192
  40.7 0.0 copy-start.5
  40.7 1.2 copy-done.5
  41.8 0.9 copy-done.14
  42.7 0.6 copy-done.22
  43.4 0.7 copy-done.23
  44.0 1.6 reduce_sum.36
  45.6 1.6 reduce_sum.37
  47.2 0.7 bitcast_add_fusion.2.coef_ref
  48.0 0.0 copy-start.6
  48.0 1.4 copy-done.6
  49.4 1.1 copy-done.15
  50.5 0.9 copy-done.17
  51.4 51.8 %exchange1.1 = (f32[2,128,128]{2,1,0:T(8,128)S(1)}, f32[2,1024,128]{2,1,0:T(8,128)S(1)}, f32[4,256,128]{2,1,0:T(8,128)S(1)}) custom-call(f32[2,128,128]{2,1,0:T(8,128)S(1)} %copy-done.17, f32[6,256,128]{2,1,0:T(8,128)S(1)} %bitcast.38, f32[3,1024,128]{2,1,0:T(8,128)S(1)} %bitcast.35, f32[2,1024,128]{2,1,0:T(8,128)S(1)} %bitcast.29), custom_call_target="tpu_custom_call" | custom-call | tf_op jit(solution)/shard_map/exchange1/pallas_call | solution.py:521
  103.3 0.0 copy-start.1
  103.3 0.0 copy-start.20
  103.3 0.0 copy-done.9
  103.3 0.0 copy-done.11
  103.3 0.0 copy-done.13
  103.3 0.0 copy-done.19
  103.3 20.7 %positions.3 = (f32[1536,128]{1,0:T(8,128)S(1)}, f32[3,8,128,128]{3,2,1,0:T(8,128)S(1)}, f32[32,8,128]{2,1,0:T(8,128)S(1)}, f32[32,8,128]{2,1,0:T(8,128)S(1)}) custom-call(s32[1]{0:T(128)} %bitcast.27.count_ref, s32[32,2]{1,0:T(8,128)S(1)} %copy-done.19, f32[32,8]{1,0:T(8,128)S(1)} %bitcast_add_fusion.2.coef_ref, f32[1024,128]{1,0:T(8,128)S(1)} %bitcast.39, ...), custom_call_target="tpu_custom_call" | custom-call | tf_op jit(solution)/shard_map/positions/pallas_call | solution.py:192
  124.0 0.0 copy-done.1
  124.0 1.2 copy-done.3
  125.2 0.1 reduce_sum.38
  125.3 0.1 reduce_sum.39
  125.4 0.8 bitcast_add_fusion
  126.2 0.7 copy.19
  126.8 1.2 copy-done.2
  128.1 1.4 copy-done.4
  129.5 0.9 copy-done.21
  130.4 44.6 %exchange2.1 = (f32[2,128,128]{2,1,0:T(8,128)S(1)}, f32[2,1024,128]{2,1,0:T(8,128)S(1)}) custom-call(f32[2,128,128]{2,1,0:T(8,128)S(1)} %copy-done.21, f32[6,256,128]{2,1,0:T(8,128)S(1)} %bitcast.37, f32[3,1024,128]{2,1,0:T(8,128)S(1)} %bitcast.34, f32[2,1024,128]{2,1,0:T(8,128)S(1)} %copy-done.2), custom_call_target="tpu_custom_call" | custom-call | tf_op jit(solution)/shard_map/exchange2/pallas_call | solution.py:521
  175.0 1.0 copy.23
  176.0 0.7 copy.27
  (17 shorter events, 0.0 us)
Async XLA Ops:
  0.6 15.6 %copy-start.7 = (bf16[768,256]{1,0:T(8,128)(2,1)S(1)}, bf16[768,256]{1,0:T(8,128)(2,1)}, u32[]{:S(2)}) copy-start(bf16[768,256]{1,0:T(8,128)(2,1)} %constant.18.fr_ref) | copy-start | bytes 1179652
  0.6 15.6 %copy-start = (s32[1,1,32,128,128]{4,3,2,1,0:T(8,128)S(1)}, s32[1,1,32,128,128]{4,3,2,1,0:T(8,128)}, u32[]{:S(2)}) copy-start(s32[1,1,32,128,128]{4,3,2,1,0:T(8,128)} %param.15) | copy-start | bytes 6291460
  4.9 0.9 copy-start.16
  16.3 1.0 copy-start.8
  17.3 1.0 copy-start.10
  18.3 1.0 copy-start.12
  19.3 0.7 copy-start.18
  40.7 1.2 copy-start.5
  41.8 0.9 copy-start.14
  42.7 0.6 copy-start.22
  43.4 0.7 copy-start.23
  48.0 1.4 copy-start.6
  49.4 1.1 copy-start.15
  50.5 0.9 copy-start.17
  51.4 51.9 %copy-start.9 = (bf16[256,768]{1,0:T(8,128)(2,1)S(1)}, bf16[256,768]{1,0:T(8,128)(2,1)}, u32[]{:S(2)}) copy-start(bf16[256,768]{1,0:T(8,128)(2,1)} %constant.23.fl_ref) | copy-start | bytes 1179652
  51.4 51.9 %copy-start.11 = (bf16[768,256]{1,0:T(8,128)(2,1)S(1)}, bf16[768,256]{1,0:T(8,128)(2,1)}, u32[]{:S(2)}) copy-start(bf16[768,256]{1,0:T(8,128)(2,1)} %constant.24.br_ref) | copy-start | bytes 1179652
  51.4 51.9 %copy-start.13 = (bf16[256,768]{1,0:T(8,128)(2,1)S(1)}, bf16[256,768]{1,0:T(8,128)(2,1)}, u32[]{:S(2)}) copy-start(bf16[256,768]{1,0:T(8,128)(2,1)} %constant.25.bl_ref) | copy-start | bytes 1179652
  51.4 51.9 %copy-start.19 = (s32[32,2]{1,0:T(8,128)S(1)}, s32[32,2]{1,0:T(8,128)}, u32[]{:S(2)}) copy-start(s32[32,2]{1,0:T(8,128)} %copy.15.offs_ref) | copy-start | bytes 772
  103.3 20.7 %copy-start.1 = (f32[2,1024,128]{2,1,0:T(8,128)}, f32[2,1024,128]{2,1,0:T(8,128)S(1)}, u32[]{:S(2)}) copy-start(f32[2,1024,128]{2,1,0:T(8,128)S(1)} %get-tuple-element.22.refs_3_) | copy-start | bytes 3145732
  103.3 20.7 %copy-start.20 = (f32[2,128,128]{2,1,0:T(8,128)}, f32[2,128,128]{2,1,0:T(8,128)S(1)}, u32[]{:S(2)}) copy-start(f32[2,128,128]{2,1,0:T(8,128)S(1)} %get-tuple-element.18.refs_0_) | copy-start | bytes 393220
  124.0 1.2 copy-start.3
  126.8 1.2 copy-start.2
  128.1 1.4 copy-start.4
  129.5 0.9 copy-start.21

commit v4 on v3

--- a/solution.py
+++ b/solution.py
@@ -11,7 +11,7 @@
 
 ITERS = 2
 GROUP = 4
-VMEM_LIMIT = 20 * 1024 * 1024
+VMEM_LIMIT = 48 * 1024 * 1024
 
 amp_floor = 0.5
 count_scale = 0.03125
@@ -211,6 +211,18 @@
     )(count, offs, coef, ext, modes, photons, *tables)
 
 
+def pack(values, upper_half):
+    size = values.shape[-1]
+    margin = size // 2
+    first, last = values[:margin], pltpu.roll(values[margin:], margin, 1)
+    upper = lax.broadcasted_iota(jnp.int32, (margin, size), 1) >= margin
+    return jnp.where(upper, first, last) if upper_half else jnp.where(upper, last, first)
+
+
+def unpack(packed):
+    return jnp.concatenate([packed, pltpu.roll(packed, packed.shape[-1] // 2, 1)], axis=0)
+
+
 def edge_copies(src_low, dst_low, src_high, dst_high, axis, sems):
     place = {name: lax.axis_index(name) for name in ("row", "col")}
     here, count = place[axis], lax.axis_size(axis)
@@ -260,10 +272,10 @@
     send_sem, recv_sem = refs[:2]
     refs = refs[2:]
     if has_halo:
-        q_s, qlow_s, qhigh_s = refs[:3]
-        refs = refs[3:]
-    if has_fold:
-        up_s, down_s, mid_s, fromlow_s, fromhigh_s, buf1, sum1, buf2, sum2, buf3 = refs
+        q_s, qsend_s, qlow_s, qhigh_s = refs[:4]
+        refs = refs[4:]
+    if has_fold:
+        up_s, down_s, mid_s, midsend_s, fromlow_s, fromhigh_s, buf1, sum1, buf2, sum2, buf3 = refs
 
     row, col = lax.axis_index("row"), lax.axis_index("col")
     rows_n, cols_n = lax.axis_size("row"), lax.axis_size("col")
@@ -366,8 +378,10 @@
                 plane = 2 * comp + half
                 mid_s[half, comp, :margin, :] = acc_ref[plane, margin:size, :] + up_s[plane]
                 mid_s[half, comp, margin:, :] = acc_ref[plane, size:tile_end, :] + down_s[plane]
+            for half in range(2):
+                midsend_s[half, comp] = pack(mid_s[half, comp], half == 1)
         start, arrive, finish = edge_copies(
-            mid_s.at[0], fromhigh_s, mid_s.at[1], fromlow_s, "col", (send_sem, recv_sem, take(2))
+            midsend_s.at[0], fromhigh_s, midsend_s.at[1], fromlow_s, "col", (send_sem, recv_sem, take(2))
         )
         start()
         finishing.append(finish)
@@ -391,7 +405,8 @@
 
         arrive()
         parts = [
-            jnp.where(upper, mid_s[0, c] + fromlow_s[c], mid_s[1, c] + fromhigh_s[c]) for c in range(3)
+            jnp.where(upper, mid_s[0, c] + unpack(fromlow_s[c]), mid_s[1, c] + unpack(fromhigh_s[c]))
+            for c in range(3)
         ]
         for c in range(2):
             new = pltpu.roll(obj_ref[c], margin, 1) + parts[c] / (parts[2] + 1.0)
@@ -412,7 +427,12 @@
         def _():
             qhigh_s[...] = jnp.zeros_like(qhigh_s)
 
-        start, arrive, finish = edge_copies(q_s, qhigh_s, q_s, qlow_s, "col", (send_sem, recv_sem, take(2)))
+        for c in range(2):
+            qsend_s[0, c] = pack(q_s[c], True)
+            qsend_s[1, c] = pack(q_s[c], False)
+        start, arrive, finish = edge_copies(
+            qsend_s.at[0], qhigh_s, qsend_s.at[1], qlow_s, "col", (send_sem, recv_sem, take(2))
+        )
         start()
         finishing.append(finish)
 
@@ -438,8 +458,8 @@
     if has_halo:
         arrive()
         for c in range(2):
-            ext_ref[2 * c, margin:tile_end, :] = jnp.where(upper, q_s[c], qlow_s[c])
-            ext_ref[2 * c + 1, margin:tile_end, :] = jnp.where(upper, qhigh_s[c], q_s[c])
+            ext_ref[2 * c, margin:tile_end, :] = jnp.where(upper, q_s[c], unpack(qlow_s[c]))
+            ext_ref[2 * c + 1, margin:tile_end, :] = jnp.where(upper, unpack(qhigh_s[c]), q_s[c])
 
         @pl.when(row == 0)
         def _():
@@ -500,7 +520,12 @@
         sems += 4
     scratch += [pltpu.SemaphoreType.DMA((sems,))] * 2
     if has_halo:
-        scratch += [pltpu.VMEM((2, size, size), f32)] * 3
+        scratch += [
+            pltpu.VMEM((2, size, size), f32),
+            pltpu.VMEM((2, 2, margin, size), f32),
+            pltpu.VMEM((2, margin, size), f32),
+            pltpu.VMEM((2, margin, size), f32),
+        ]
     if has_fold:
         half_rows = moments.shape[1] // 2
         lines = rows_n // 2
@@ -510,8 +535,9 @@
             pltpu.VMEM((6, margin, size), f32),
             pltpu.VMEM((6, margin, size), f32),
             pltpu.VMEM((2, 3, size, size), f32),
-            pltpu.VMEM((3, size, size), f32),
-            pltpu.VMEM((3, size, size), f32),
+            pltpu.VMEM((2, 3, margin, size), f32),
+            pltpu.VMEM((3, margin, size), f32),
+            pltpu.VMEM((3, margin, size), f32),
             pltpu.VMEM((3, half_rows, size), f32),
             pltpu.VMEM((3, half_rows, size), f32),
             pltpu.VMEM((max(lines - 1, 1), 3, line_rows, size), f32),

time: 179 us -> 162 us (0.905); the launches traced: 177 us -> 162 us
  local copies, waits for them, and re-layouts: 22.1 us -> 12.7 us
  other arithmetic: 4.92 us -> 0.44 us
    unnamed x52 -> x34, local copies, waits for them, and re-layouts: 19.7 us -> 11.5 us
    reduce_sum x4, other arithmetic: 3.42 us -> 0.41 us  [shards(): coef = coef + num.sum(axis=-1) / (den.sum(axis=-1) + 1.0)]
    pallas_call x3, Pallas kernels: 107 us -> 105 us  [exchange_call(): pl.pallas_call(functools.partial(exchange_kernel, has_fold, has_halo), ou...]
where the time goes in v4:
time: 162 us
  Pallas kernels  147 us (91%)
  local copies, waits for them, and re-layouts  12.7 us (8%)
    pallas_call x3, Pallas kernels, exchange_call(): pl.pallas_call(functools.partial(exchange_kernel, has_fold, has_halo), ou...  105 us
    pallas_call x2, Pallas kernels, positions_call(): pl.pallas_call(positions_kernel, out_shape=(jax.ShapeDtypeStruct((6 * ext...  42.4 us
    unnamed x34, local copies, waits for them, and re-layouts  11.5 us

profile of v4, /device:TPU:5, one launch (start us, length us, event | category | flops | bytes accessed | tf_op | source)
XLA Modules:
  0.0 161.6 jit_solution(12265517114390382187)
XLA Ops:
  0.6 0.0 copy-start.4
  0.6 0.0 copy-start.5
  0.7 0.0 copy-start.6
  0.7 0.0 copy-start.7
  0.7 0.0 copy-start.14
  0.7 0.0 copy-start.11
  0.7 0.9 copy.13
  1.6 1.3 copy.24
  2.9 0.0 copy-done.14
  2.9 0.1 copy.15.offs_ref
  3.6 0.0 copy-done.11
  3.6 9.3 %exchange0.1 = f32[4,256,128]{2,1,0:T(8,128)S(1)} custom-call(f32[2,128,128]{2,1,0:T(8,128)S(1)} %copy-done.11), custom_call_target="tpu_custom_call" | custom-call | tf_op jit(solution)/shard_map/exchange0/pallas_call | solution.py:547
  13.0 0.0 copy-done.4
  13.0 0.0 copy-done.5
  13.0 0.0 copy-done.6
  13.0 0.0 copy-done.7
  13.0 21.2 %positions.2 = (f32[1536,128]{1,0:T(8,128)S(1)}, f32[3,8,128,128]{3,2,1,0:T(8,128)S(1)}, f32[32,8,128]{2,1,0:T(8,128)S(1)}, f32[32,8,128]{2,1,0:T(8,128)S(1)}) custom-call(s32[1]{0:T(128)} %bitcast.26.count_ref, s32[32,2]{1,0:T(8,128)S(1)} %copy.15.offs_ref, f32[32,8]{1,0:T(8,128)S(1)} %bitcast.38, f32[1024,128]{1,0:T(8,128)S(1)} %bitcast.31, ...), custom_call_target="tpu_custom_call" | custom-call | tf_op jit(solution)/shard_map/positions/pallas_call | solution.py:192
  34.2 0.0 copy-start.2
  34.2 1.1 copy-done.2
  35.3 0.0 copy-start.9
  35.3 0.9 copy-done.9
  36.2 0.1 reduce_sum.36
  36.3 0.1 reduce_sum.37
  36.4 0.0 copy-start.3
  36.5 1.4 copy-done.3
  37.9 0.0 copy-start.10
  37.9 1.1 copy-done.10
  39.0 0.0 copy-start.8
  39.0 48.2 %exchange1.1 = (f32[2,128,128]{2,1,0:T(8,128)S(1)}, f32[2,1024,128]{2,1,0:T(8,128)S(1)}, f32[4,256,128]{2,1,0:T(8,128)S(1)}) custom-call(f32[2,128,128]{2,1,0:T(8,128)S(1)} %copy-done.11, f32[6,256,128]{2,1,0:T(8,128)S(1)} %bitcast.36, f32[3,1024,128]{2,1,0:T(8,128)S(1)} %bitcast.33, f32[2,1024,128]{2,1,0:T(8,128)S(1)} %bitcast.29), custom_call_target="tpu_custom_call" | custom-call | tf_op jit(solution)/shard_map/exchange1/pallas_call | solution.py:547
  87.2 0.0 copy-start.12
  87.2 0.0 copy-done.8
  87.2 21.2 %positions.3 = (f32[1536,128]{1,0:T(8,128)S(1)}, f32[3,8,128,128]{3,2,1,0:T(8,128)S(1)}, f32[32,8,128]{2,1,0:T(8,128)S(1)}, f32[32,8,128]{2,1,0:T(8,128)S(1)}) custom-call(s32[1]{0:T(128)} %bitcast.27.count_ref, s32[32,2]{1,0:T(8,128)S(1)} %copy.15.offs_ref, f32[32,8]{1,0:T(8,128)S(1)} %bitcast_add_fusion.2.coef_ref, f32[1024,128]{1,0:T(8,128)S(1)} %bitcast.37, ...), custom_call_target="tpu_custom_call" | custom-call | tf_op jit(solution)/shard_map/positions/pallas_call | solution.py:192
  108.4 0.0 copy-done.12
  108.4 0.0 copy-start
  108.5 1.1 copy-done
  109.6 0.1 reduce_sum.38
  109.7 0.1 reduce_sum.39
  109.8 0.7 copy.19
  110.5 0.0 copy-start.1
  110.5 1.4 copy-done.1
  111.9 0.0 copy-start.13
  111.9 0.9 copy-done.13
  112.8 47.1 %exchange2.1 = (f32[2,128,128]{2,1,0:T(8,128)S(1)}, f32[2,1024,128]{2,1,0:T(8,128)S(1)}) custom-call(f32[2,128,128]{2,1,0:T(8,128)S(1)} %copy-done.13, f32[6,256,128]{2,1,0:T(8,128)S(1)} %bitcast.35, f32[3,1024,128]{2,1,0:T(8,128)S(1)} %bitcast.32, f32[2,1024,128]{2,1,0:T(8,128)S(1)} %get-tuple-element.22.refs_3_), custom_call_target="tpu_custom_call" | custom-call | tf_op jit(solution)/shard_map/exchange2/pallas_call | solution.py:547
  159.9 1.1 copy.23
  161.0 0.7 copy.27
  (2 shorter events, 0.0 us)
Async XLA Ops:
  0.6 12.3 %copy-start.4 = (bf16[768,256]{1,0:T(8,128)(2,1)S(1)}, bf16[768,256]{1,0:T(8,128)(2,1)}, u32[]{:S(2)}) copy-start(bf16[768,256]{1,0:T(8,128)(2,1)} %constant.18.fr_ref) | copy-start | bytes 1179652
  0.6 12.3 %copy-start.5 = (bf16[256,768]{1,0:T(8,128)(2,1)S(1)}, bf16[256,768]{1,0:T(8,128)(2,1)}, u32[]{:S(2)}) copy-start(bf16[256,768]{1,0:T(8,128)(2,1)} %constant.23.fl_ref) | copy-start | bytes 1179652
  0.7 12.3 %copy-start.6 = (bf16[768,256]{1,0:T(8,128)(2,1)S(1)}, bf16[768,256]{1,0:T(8,128)(2,1)}, u32[]{:S(2)}) copy-start(bf16[768,256]{1,0:T(8,128)(2,1)} %constant.24.br_ref) | copy-start | bytes 1179652
  0.7 12.3 %copy-start.7 = (bf16[256,768]{1,0:T(8,128)(2,1)S(1)}, bf16[256,768]{1,0:T(8,128)(2,1)}, u32[]{:S(2)}) copy-start(bf16[256,768]{1,0:T(8,128)(2,1)} %constant.25.bl_ref) | copy-start | bytes 1179652
  0.7 2.2 %copy-start.14 = (s32[1,1,32,2]{2,3,1,0:T(2,128)S(1)}, s32[1,1,32,2]{2,3,1,0:T(2,128)}, u32[]{:S(2)}) copy-start(s32[1,1,32,2]{2,3,1,0:T(2,128)} %param.13) | copy-start | bytes 772
  0.7 2.9 %copy-start.11 = (f32[2,128,128]{2,1,0:T(8,128)S(1)}, f32[2,128,128]{2,1,0:T(8,128)}, u32[]{:S(2)}) copy-start(f32[2,128,128]{2,1,0:T(8,128)} %refs_0_.3) | copy-start | bytes 393220
  34.2 1.1 copy-start.2
  35.3 0.9 copy-start.9
  36.4 1.4 copy-start.3
  37.9 1.1 copy-start.10
  39.0 48.2 %copy-start.8 = (bf16[256,768]{1,0:T(8,128)(2,1)S(1)}, bf16[256,768]{1,0:T(8,128)(2,1)}, u32[]{:S(2)}) copy-start(bf16[256,768]{1,0:T(8,128)(2,1)} %constant.25.bl_ref) | copy-start | bytes 1179652
  87.2 21.2 %copy-start.12 = (f32[2,128,128]{2,1,0:T(8,128)}, f32[2,128,128]{2,1,0:T(8,128)S(1)}, u32[]{:S(2)}) copy-start(f32[2,128,128]{2,1,0:T(8,128)S(1)} %get-tuple-element.18.refs_0_) | copy-start | bytes 393220
  108.4 1.1 copy-start
  110.5 1.4 copy-start.1
  111.9 0.9 copy-start.13
